TPU v7x, 32 devices: a whole 2x2x4 slice. The times are simulated.
32 devices in a mesh: xy: 16 (over z, y, x), gz: 2 (over core).
Axes of the slice: x: 2, y: 2, z: 4, core: 2. Of those that a mesh axis runs over, the one named last changes fastest.
Arguments:
- potential_temp: float32 [4, 64, 512], P('gz', 'xy'), may hold values from -6 to 6
- wind_field: float32 [3, 4, 64, 512], P(None, 'gz', 'xy'), may hold values from -0.25 to 0.25
- eddy_diff: float32 [4, 64, 512], P('gz', 'xy'), may hold values from 0.005 to 0.04
- facade_cell: int32 [2, 2048, 128], P('gz', 'xy'), may hold values from 0 to 4095
- tile_send: int32 [2, 2048], P('gz', 'xy'), may hold values from -1 to 127, as said below
- tile_take: int32 [2, 1024], P('gz', 'xy'), may hold values from 0 to 127, as said below
- wall_temp: float32 [2, 1024, 32, 128], P('gz', 'xy'), may hold values from -6 to 6
- wall_class: int32 [2, 1024], P('gz', 'xy'), may hold values from 0 to 3
- wall_inverse: float32 [4, 32, 32], replicated, as said below
- refl_block: bfloat16 [16, 32, 128, 128], P('xy', 'gz'), may hold values from -0.5 to 0.5
- refl_pair: int32 [16, 2, 32], P('xy', None, 'gz'), may hold values from 0 to 127
Outputs:
- temp_next: float32 [4, 64, 512], P('gz', 'xy')
- wall_next: float32 [2, 1024, 32, 128], P('gz', 'xy')
Inputs may be any that keep to these rules, and one draw needn't show every extreme that they name: `tile_send`: in each vertical index, each LES device's live slots carry distinct values dest * 8 + c with c below the number of tiles that it sends to owner dest, and at most 8 tiles go from one LES device to one owner; some LES device has all 128 slots live, with 8 tiles to every owner, and empty slots hold -1. `tile_take`: for owner j at vertical index k, the 64 values are exactly the rows src * 8 + c for which LES device src sends a tile with value j * 8 + c, each once; every owner receives exactly 64 tiles. `wall_inverse`: nonnegative entries, diagonally dominant by rows.
All inputs are finite; a program needn't handle non-finite values.
Results may differ from a plain program's by a relative error of at most 0.0014.
Values may be sent and summed in bfloat16 or wider, within the bound.
A program may use at most 64 MiB of HBM per device.

v0:
```python
import jax
import jax.numpy as jnp
from jax import lax
from jax.sharding import PartitionSpec as P

SUB = 4


wall_gain = 0.25
flux_gain = 0.5


def with_halo(array, sides, width):
    for axis, dim in sides:
        size, length = (lax.axis_size(axis), array.shape[dim])
        up = [(i, (i + 1) % size) for i in range(size - 1)]
        down = [(j, i) for i, j in up]
        last = lax.slice_in_dim(array, length - width, length, axis=dim)
        initial = lax.slice_in_dim(array, 0, width, axis=dim)
        before = lax.ppermute(last, axis, up)
        after = lax.ppermute(initial, axis, down)
        array = jnp.concatenate([before, array, after], axis=dim)
    return array


def upwind(speed, centre, lower, upper):
    return jnp.maximum(speed, 0.0) * (centre - lower) + jnp.minimum(speed, 0.0) * (upper - centre)


def on_device(
    potential_temp,
    wind_field,
    eddy_diff,
    facade_cell,
    tile_send,
    tile_take,
    wall_temp,
    wall_class,
    wall_inverse,
    refl_block,
    refl_pair,
):
    levels, x_rows, y_cells = potential_temp.shape
    tile_slots = facade_cell.shape[1]
    tile_width = facade_cell.shape[2]
    owned = tile_take.shape[1]
    node_count = wall_temp.shape[2]
    xy_count = lax.axis_size("xy")
    capacity = 2 * owned // xy_count
    slot_total = xy_count * capacity
    speed_sq = (
        wind_field[0] * wind_field[0]
        + wind_field[1] * wind_field[1]
        + wind_field[2] * wind_field[2]
    )
    line_count = levels * x_rows
    both_lines = jnp.concatenate(
        (potential_temp.reshape(line_count, y_cells), speed_sq.reshape(line_count, y_cells)), axis=0
    )
    facade_total = tile_slots * tile_width
    block_size = min(2048, facade_total // 8)
    block_count = facade_total // block_size
    cell_index = facade_cell.reshape(facade_total)
    index_blocks = cell_index.reshape(block_count, block_size)
    lane_ids = lax.broadcasted_iota(jnp.int32, (1, y_cells), 1)
    line_lanes = lax.broadcasted_iota(jnp.int32, (1, line_count), 1)

    def factors(index_block):
        line_hot = ((index_block // y_cells)[:, None] == line_lanes).astype(jnp.float32)
        column_hot = ((index_block % y_cells)[:, None] == lane_ids).astype(jnp.float32)
        return (line_hot, column_hot)

    def lookup(index_block):
        line_hot, column_hot = factors(index_block)
        picked = lax.dot_general(
            column_hot,
            both_lines,
            (((1,), (1,)), ((), ())),
            precision=lax.Precision.HIGHEST,
            preferred_element_type=jnp.float32,
        )
        theta_val = jnp.sum(picked[:, :line_count] * line_hot, axis=1)
        speed_val = jnp.sum(picked[:, line_count:] * line_hot, axis=1)
        return (theta_val, speed_val)

    theta_found, speed_found = lax.map(lookup, index_blocks)
    air_slots = theta_found.reshape(tile_slots, tile_width)
    coef_slots = 0.5 + 4.0 * speed_found.reshape(tile_slots, tile_width)
    send_rows = tile_send.reshape(tile_slots)
    target_rows = jnp.where(send_rows >= 0, send_rows, slot_total)
    empty_box = jnp.zeros((slot_total + 1, tile_width), jnp.float32)
    air_out = empty_box.at[target_rows].set(air_slots)[:slot_total]
    coef_out = empty_box.at[target_rows].set(coef_slots)[:slot_total]
    air_recv, coef_recv = (
        lax.all_to_all(air_out, "xy", split_axis=0, concat_axis=0, tiled=True),
        lax.all_to_all(coef_out, "xy", split_axis=0, concat_axis=0, tiled=True),
    )
    take_rows = tile_take.reshape(owned)
    own_air = air_recv[take_rows]
    own_coef = coef_recv[take_rows]
    wall_state = wall_temp.reshape(owned, node_count, tile_width)
    emitted = wall_state[:, 0, :].astype(jnp.bfloat16)
    district = lax.all_gather(emitted, "gz", axis=0, tiled=True)
    blocks = refl_block[0]
    pair_rows = refl_pair[0]
    source_emit = district[pair_rows[1]]
    contrib = jnp.einsum("bij,bj->bi", blocks, source_emit, preferred_element_type=jnp.float32)
    targets = pair_rows[0]
    district_rows = lax.axis_size("gz") * owned
    row_ids = lax.iota(jnp.int32, district_rows)
    one_hot = (row_ids[:, None] == targets[None, :]).astype(jnp.float32)
    whole = lax.psum(
        jnp.dot(
            one_hot, contrib, precision=lax.Precision.HIGHEST, preferred_element_type=jnp.float32
        ).astype(jnp.bfloat16),
        "gz",
    ).astype(jnp.float32)
    own_rad = lax.dynamic_slice_in_dim(whole, lax.axis_index("gz") * owned, owned, 0)
    class_ids = lax.broadcasted_iota(jnp.int32, (owned, wall_inverse.shape[0]), 1)
    class_hot = (wall_class.reshape(owned)[:, None] == class_ids).astype(jnp.float32)
    inverse_tile = jnp.einsum(
        "tc,cab->tab", class_hot, wall_inverse, precision=lax.Precision.HIGHEST
    )
    temps = wall_state
    for substep in range(SUB):
        forcing = own_coef * (own_air - temps[:, 0, :]) + own_rad
        temps = temps.at[:, 0, :].add(wall_gain * forcing)
        temps = jnp.einsum("tab,tbf->taf", inverse_tile, temps, precision=lax.Precision.HIGHEST)
    flux_out = own_coef * (temps[:, 0, :] - own_air)
    back_rows = jnp.zeros((slot_total, tile_width), jnp.float32).at[take_rows].set(flux_out)
    returned = lax.all_to_all(back_rows, "xy", split_axis=0, concat_axis=0, tiled=True)
    slot_flux = returned[jnp.maximum(send_rows, 0)]
    slot_flux = jnp.where((send_rows >= 0)[:, None], slot_flux, 0.0)
    flux_blocks = slot_flux.reshape(block_count, block_size)

    def deposit(total, inputs):
        index_block, flux_block = inputs
        line_hot, column_hot = factors(index_block)
        weighted = column_hot * flux_block[:, None]
        added = lax.dot_general(
            line_hot,
            weighted,
            (((0,), (0,)), ((), ())),
            precision=lax.Precision.HIGHEST,
            preferred_element_type=jnp.float32,
        )
        return (total + added, None)

    heat_lines, unused = lax.scan(
        deposit, jnp.zeros((line_count, y_cells), jnp.float32), (index_blocks, flux_blocks)
    )
    heat_cells = heat_lines.reshape(levels, x_rows, y_cells)
    padded = with_halo(potential_temp, (("xy", 1), ("gz", 0)), 1)
    lower_z = padded[:-2, 1:-1]
    upper_z = padded[2:, 1:-1]
    lower_x = padded[1:-1, :-2]
    upper_x = padded[1:-1, 2:]
    lower_y = jnp.roll(potential_temp, 1, axis=2)
    upper_y = jnp.roll(potential_temp, -1, axis=2)
    advect = (
        upwind(wind_field[0], potential_temp, lower_z, upper_z)
        + upwind(wind_field[1], potential_temp, lower_x, upper_x)
        + upwind(wind_field[2], potential_temp, lower_y, upper_y)
    )
    laplace = lower_z + upper_z + lower_x + upper_x + lower_y + upper_y - 6.0 * potential_temp
    temp_next = potential_temp - advect + eddy_diff * laplace + flux_gain * heat_cells
    return (temp_next, temps.reshape(1, owned, node_count, tile_width))


def solution(mesh):
    in_specs = (
        P("gz", "xy", None),
        P(None, "gz", "xy", None),
        P("gz", "xy", None),
        P("gz", "xy", None),
        P("gz", "xy"),
        P("gz", "xy"),
        P("gz", "xy", None, None),
        P("gz", "xy"),
        P(),
        P("xy", "gz", None, None),
        P("xy", None, "gz"),
    )
    out_specs = (P("gz", "xy", None), P("gz", "xy", None, None))
    return jax.shard_map(
        on_device, mesh=mesh, in_specs=in_specs, out_specs=out_specs, check_vma=False
    )
```

profile of v0, /device:TPU:0, one launch (start us, length us, event | category | flops | bytes accessed | tf_op | source)
XLA Modules:
  0.0 107.5 jit_solution(9156509238448280464)
XLA Ops:
  0.7 0.9 reshape_reshape.3
  1.6 0.8 multiply_add_fusion.1
  2.4 0.7 reshape.393
  3.1 21.8 %while.34 = (s32[]{:T(128)}, f32[8,2048]{1,0:T(8,128)S(1)}, f32[8,2048]{1,0:T(8,128)S(1)}, s32[8,2048]{1,0:T(8,128)S(1)}, f32[16,512]{1,0:T(8,128)S(1)}) while((s32[]{:T(128)}, f32[8,2048]{1,0:T(8,128)S(1)}, f32[8,2048]{1,0:T(8,128)S(1)}, s32[8,2048]{1,0:T(8,128)S(1)}, f32[16,512]{1,0:T(8,128)S(1)}) %tuple.99), condition=%wide.region_3.4_spmd.clone.clone, body=%wide.region_0.3_spmd.clone.sunk.clone | while | flops 202491904 | bytes 401481 | solution.py:86
  3.2 2.2 %fusion.109 = f32[2048,16]{0,1:T(8,128)S(1)} fusion(f32[16,512]{1,0:T(8,128)S(1)} %get-tuple-element.406, s32[2048]{0:T(1024)S(1)} %get-tuple-element.368), kind=kOutput, calls=%fused_computation.12.clone.1.clone | convolution fusion | flops 202375168 | bytes 172032 | tf_op jit(solution)/shard_map/while/body/eval_jaxpr/dot_general | solution.py:75
  5.4 0.2 dynamic_update_slice.20
  5.6 0.2 dynamic_update_slice.19
  5.9 2.2 %fusion.109 = f32[2048,16]{0,1:T(8,128)S(1)} fusion(f32[16,512]{1,0:T(8,128)S(1)} %get-tuple-element.406, s32[2048]{0:T(1024)S(1)} %get-tuple-element.368), kind=kOutput, calls=%fused_computation.12.clone.1.clone | convolution fusion | flops 202375168 | bytes 172032 | tf_op jit(solution)/shard_map/while/body/eval_jaxpr/dot_general | solution.py:75
  8.2 0.2 dynamic_update_slice.20
  8.4 0.2 dynamic_update_slice.19
  8.6 2.2 %fusion.109 = f32[2048,16]{0,1:T(8,128)S(1)} fusion(f32[16,512]{1,0:T(8,128)S(1)} %get-tuple-element.406, s32[2048]{0:T(1024)S(1)} %get-tuple-element.368), kind=kOutput, calls=%fused_computation.12.clone.1.clone | convolution fusion | flops 202375168 | bytes 172032 | tf_op jit(solution)/shard_map/while/body/eval_jaxpr/dot_general | solution.py:75
  10.9 0.2 dynamic_update_slice.20
  11.1 0.2 dynamic_update_slice.19
  11.4 2.2 %fusion.109 = f32[2048,16]{0,1:T(8,128)S(1)} fusion(f32[16,512]{1,0:T(8,128)S(1)} %get-tuple-element.406, s32[2048]{0:T(1024)S(1)} %get-tuple-element.368), kind=kOutput, calls=%fused_computation.12.clone.1.clone | convolution fusion | flops 202375168 | bytes 172032 | tf_op jit(solution)/shard_map/while/body/eval_jaxpr/dot_general | solution.py:75
  13.6 0.2 dynamic_update_slice.20
  13.8 0.2 dynamic_update_slice.19
  14.1 2.2 %fusion.109 = f32[2048,16]{0,1:T(8,128)S(1)} fusion(f32[16,512]{1,0:T(8,128)S(1)} %get-tuple-element.406, s32[2048]{0:T(1024)S(1)} %get-tuple-element.368), kind=kOutput, calls=%fused_computation.12.clone.1.clone | convolution fusion | flops 202375168 | bytes 172032 | tf_op jit(solution)/shard_map/while/body/eval_jaxpr/dot_general | solution.py:75
  16.3 0.2 dynamic_update_slice.20
  16.8 2.2 %fusion.109 = f32[2048,16]{0,1:T(8,128)S(1)} fusion(f32[16,512]{1,0:T(8,128)S(1)} %get-tuple-element.406, s32[2048]{0:T(1024)S(1)} %get-tuple-element.368), kind=kOutput, calls=%fused_computation.12.clone.1.clone | convolution fusion | flops 202375168 | bytes 172032 | tf_op jit(solution)/shard_map/while/body/eval_jaxpr/dot_general | solution.py:75
  19.5 2.2 %fusion.109 = f32[2048,16]{0,1:T(8,128)S(1)} fusion(f32[16,512]{1,0:T(8,128)S(1)} %get-tuple-element.406, s32[2048]{0:T(1024)S(1)} %get-tuple-element.368), kind=kOutput, calls=%fused_computation.12.clone.1.clone | convolution fusion | flops 202375168 | bytes 172032 | tf_op jit(solution)/shard_map/while/body/eval_jaxpr/dot_general | solution.py:75
  22.3 2.2 %fusion.109 = f32[2048,16]{0,1:T(8,128)S(1)} fusion(f32[16,512]{1,0:T(8,128)S(1)} %get-tuple-element.406, s32[2048]{0:T(1024)S(1)} %get-tuple-element.368), kind=kOutput, calls=%fused_computation.12.clone.1.clone | convolution fusion | flops 202375168 | bytes 172032 | tf_op jit(solution)/shard_map/while/body/eval_jaxpr/dot_general | solution.py:75
  25.0 0.9 scatter_custom_fusion
  25.9 0.6 slice_bitcast_fusion.1
  26.5 8.3 %all-to-all-start = ((f32[16,8,128]{2,1,0:T(8,128)}), f32[16,8,128]{2,1,0:T(8,128)S(1)}, u32[]{:S(2)}, u32[]{:S(2)}) async-start(f32[16,8,128]{2,1,0:T(8,128)} %slice_bitcast_fusion.1), calls=%async_computation | async-start | bytes 131072 | tf_op jit(solution)/shard_map/all_to_all | solution.py:96
  34.9 3.8 %collective-permute-start = (f32[2,1,512]{2,1,0:T(1,128)S(1)}, f32[2,1,512]{2,1,0:T(1,128)S(1)}, u32[]{:S(2)}, u32[]{:S(2)}) collective-permute-start(f32[2,1,512]{2,1,0:T(1,128)S(1)} %get-tuple-element.290), channel_id=1, source_target_pairs={{0,2},{2,4},{4,6},{6,8},{8,10},{10,12},{12,14},{14,16},{16,18},{18... | collective-permute-start | bytes 12296 | tf_op jit(solution)/shard_map/ppermute | solution.py:20
  38.7 1.3 %collective-permute-start.1 = (f32[2,1,512]{2,1,0:T(1,128)S(1)}, f32[2,1,512]{2,1,0:T(1,128)S(1)}, u32[]{:S(2)}, u32[]{:S(2)}) collective-permute-start(f32[2,1,512]{2,1,0:T(1,128)S(1)} %get-tuple-element.291), channel_id=1, source_target_pairs={{2,0},{4,2},{6,4},{8,6},{10,8},{12,10},{14,12},{16,14},{18,16},{20... | collective-permute-start | bytes 12296 | tf_op jit(solution)/shard_map/ppermute | solution.py:21
  40.0 0.6 copy.41
  40.9 0.9 scatter_custom_fusion.1
  41.8 0.6 slice_bitcast_fusion
  42.4 1.8 %all_gather.3 = bf16[128,128]{1,0:T(8,128)(2,1)S(1)} all-gather(bf16[64,128]{1,0:T(8,128)(2,1)S(1)} %fusion.54), channel_id=1, replica_groups=mesh['xy'=16,'gz'=2] {'gz'}, dimensions={0}, use_global_device_ids=true | all-gather | bytes 49152 | tf_op jit(solution)/shard_map/all_gather | solution.py:103
  44.2 0.6 gather_fusion.2
  44.8 0.4 fusion.28
  45.4 0.6 fusion.30
  46.0 7.6 %all-to-all-start.1 = ((f32[16,8,128]{2,1,0:T(8,128)}), f32[16,8,128]{2,1,0:T(8,128)S(1)}, u32[]{:S(2)}, u32[]{:S(2)}) async-start(f32[16,8,128]{2,1,0:T(8,128)} %slice_bitcast_fusion), calls=%async_computation.1 | async-start | bytes 131072 | tf_op jit(solution)/shard_map/all_to_all | solution.py:95
  53.7 3.4 %psum.7 = bf16[128,128]{1,0:T(8,128)(2,1)S(1)} all-reduce(bf16[128,128]{1,0:T(8,128)(2,1)S(1)} %convolution_convert_fusion), channel_id=1, replica_groups=mesh['xy'=16,'gz'=2] {'gz'}, use_global_device_ids=true, to_apply=%region_6.7 | all-reduce | flops 16384 | bytes 65536 | tf_op jit(solution)/shard_map/psum | solution.py:112
  57.1 1.0 copy.53
  58.1 0.9 copy.27
  59.2 0.6 gather_fusion
  59.8 1.4 %all-to-all-done.1 = f32[16,8,128]{2,1,0:T(8,128)S(1)} async-done(((f32[16,8,128]{2,1,0:T(8,128)}), f32[16,8,128]{2,1,0:T(8,128)S(1)}, u32[]{:S(2)}, u32[]{:S(2)}) %all-to-all-start.1) | async-done | bytes 65568 | tf_op jit(solution)/shard_map/all_to_all | solution.py:95
  61.2 0.6 gather_fusion.1
  61.8 0.6 fusion.42
  62.5 2.9 %fusion.26 = f32[64,32,128]{2,1,0:T(8,128)S(1)} fusion(f32[64,32,32]{2,1,0:T(8,128)S(1)} %copy.27, f32[64,32,128]{2,0,1:T(8,128)} %fusion.42), kind=kOutput, calls=%fused_computation.49 | convolution fusion | flops 100663296 | bytes 2359296 | tf_op jit(solution)/shard_map/tab,tbf->taf/dot_general | solution.py:128
  65.6 1.2 %fusion.86 = f32[64,32,128]{2,1,0:T(8,128)S(1)} fusion(f32[64,32,32]{2,1,0:T(8,128)S(1)} %copy.27, f32[64,32,128]{2,1,0:T(8,128)S(1)} %scatter-add.15), kind=kOutput, calls=%fused_computation.149 | convolution fusion | flops 100663296 | bytes 2359296 | tf_op jit(solution)/shard_map/tab,tbf->taf/dot_general | solution.py:128
  66.8 1.0 copy-done.1
  67.9 1.7 %scatter-add.16 = f32[64,32,128]{2,1,0:T(8,128)} dynamic-update-slice(f32[64,32,128]{2,1,0:T(8,128)} %copy-done.1, f32[64,1,128]{2,1,0:T(1,128)S(1)} %bitcast.156, s32[]{:T(128)} %copy.64, s32[]{:T(128)} %copy.64, s32[]{:T(128)} %copy.64) | dynamic-update-slice | bytes 65540 | tf_op jit(solution)/shard_map/scatter-add | solution.py:127
  69.6 2.4 %fusion.87 = f32[64,32,128]{2,1,0:T(8,128)S(1)} fusion(f32[64,32,32]{2,1,0:T(8,128)S(1)} %copy.27, f32[64,32,128]{2,1,0:T(8,128)} %scatter-add.16), kind=kOutput, calls=%fused_computation.150 | convolution fusion | flops 100663296 | bytes 2359296 | tf_op jit(solution)/shard_map/tab,tbf->taf/dot_general | solution.py:128
  72.2 1.2 %fusion.88 = f32[64,32,128]{2,1,0:T(8,128)S(1)} fusion(f32[64,32,32]{2,1,0:T(8,128)S(1)} %copy.27, f32[64,32,128]{2,1,0:T(8,128)S(1)} %scatter-add.19), kind=kOutput, calls=%fused_computation.151 | convolution fusion | flops 100663296 | bytes 2359296 | tf_op jit(solution)/shard_map/tab,tbf->taf/dot_general | solution.py:128
  73.4 1.0 copy-done.2
  74.4 1.3 %scatter_custom_fusion.2 = f32[128,128]{1,0:T(8,128)} fusion(s32[64]{0:T(128)S(1)} %fusion.77, f32[64,128]{1,0:T(8,128)S(1)} %gather_fusion, f32[64,128]{1,0:T(8,128)S(1)} %bitcast.153, f32[64,128]{1,0:T(8,128)S(1)} %gather_fusion.1, f32[]{:T(128)} %constant.233.clone.1), kind=kCustom, calls=%fused_computation.85 | custom fusion | flops 16384 | bytes 163844 | tf_op jit(solution)/shard_map/scatter | solution.py:130
  75.7 5.5 %all-to-all-start.2 = ((f32[16,8,128]{2,1,0:T(8,128)}), f32[16,8,128]{2,1,0:T(8,128)S(1)}, u32[]{:S(2)}, u32[]{:S(2)}) async-start(f32[16,8,128]{2,1,0:T(8,128)} %bitcast.38), calls=%async_computation.2 | async-start | bytes 131072 | tf_op jit(solution)/shard_map/all_to_all | solution.py:131
  81.2 2.0 %collective-permute-start.2 = (f32[1,6,512]{2,1,0:T(8,128)S(1)}, f32[1,6,512]{2,1,0:T(8,128)S(1)}, u32[]{:S(2)}, u32[]{:S(2)}) collective-permute-start(f32[1,6,512]{2,1,0:T(8,128)S(1)} %get-tuple-element.284), channel_id=1, source_target_pairs={{0,1},{2,3},{4,5},{6,7},{8,9},{10,11},{12,13},{14,15},{16,17},{18,... | collective-permute-start | bytes 36872 | tf_op jit(solution)/shard_map/ppermute | solution.py:20
  83.2 1.3 %collective-permute-start.3 = (f32[1,6,512]{2,1,0:T(8,128)S(1)}, f32[1,6,512]{2,1,0:T(8,128)S(1)}, u32[]{:S(2)}, u32[]{:S(2)}) collective-permute-start(f32[1,6,512]{2,1,0:T(8,128)S(1)} %get-tuple-element.285), channel_id=1, source_target_pairs={{1,0},{3,2},{5,4},{7,6},{9,8},{11,10},{13,12},{15,14},{17,16},{19,... | collective-permute-start | bytes 36872 | tf_op jit(solution)/shard_map/ppermute | solution.py:21
  84.5 4.2 %all-to-all-done.2 = f32[16,8,128]{2,1,0:T(8,128)S(1)} async-done(((f32[16,8,128]{2,1,0:T(8,128)}), f32[16,8,128]{2,1,0:T(8,128)S(1)}, u32[]{:S(2)}, u32[]{:S(2)}) %all-to-all-start.2) | async-done | bytes 65568 | tf_op jit(solution)/shard_map/all_to_all | solution.py:131
  88.8 0.6 gather_fusion.3
  89.5 17.2 %while.35 = (s32[]{:T(128)}, f32[8,512]{1,0:T(8,128)S(1)}, s32[8,2048]{1,0:T(8,128)S(1)}, f32[8,2048]{1,0:T(8,128)S(1)}) while((s32[]{:T(128)}, f32[8,512]{1,0:T(8,128)S(1)}, s32[8,2048]{1,0:T(8,128)S(1)}, f32[8,2048]{1,0:T(8,128)S(1)}) %tuple.105), condition=%wide.region_9.10_spmd.clone.clone, body=%wide.region_8.9_spmd.clone.sunk.clone | while | flops 102823936 | bytes 114759 | solution.py:149
  89.6 2.1 %fusion.112 = f32[8,512]{1,0:T(8,128)S(1)} fusion(f32[2048]{0:T(1024)S(1)} %bitcast.152, s32[2048]{0:T(1024)S(1)} %get-tuple-element.384, s32[2048]{0:T(1024)S(1)} %get-tuple-element.385, f32[8,512]{1,0:T(8,128)S(1)} %get-tuple-element.412, pred[]{:T(512)S(6)} %compare.49), kind=kOutput, calls=%fused_computation.34.clone.1.clone | convolution fusion | flops 102785024 | bytes 57345 | tf_op jit(solution)/shard_map/while/body/eval_jaxpr/dot_general | solution.py:140
  91.8 2.1 %fusion.112 = f32[8,512]{1,0:T(8,128)S(1)} fusion(f32[2048]{0:T(1024)S(1)} %bitcast.152, s32[2048]{0:T(1024)S(1)} %get-tuple-element.384, s32[2048]{0:T(1024)S(1)} %get-tuple-element.385, f32[8,512]{1,0:T(8,128)S(1)} %get-tuple-element.412, pred[]{:T(512)S(6)} %compare.49), kind=kOutput, calls=%fused_computation.34.clone.1.clone | convolution fusion | flops 102785024 | bytes 57345 | tf_op jit(solution)/shard_map/while/body/eval_jaxpr/dot_general | solution.py:140
  93.9 2.1 %fusion.112 = f32[8,512]{1,0:T(8,128)S(1)} fusion(f32[2048]{0:T(1024)S(1)} %bitcast.152, s32[2048]{0:T(1024)S(1)} %get-tuple-element.384, s32[2048]{0:T(1024)S(1)} %get-tuple-element.385, f32[8,512]{1,0:T(8,128)S(1)} %get-tuple-element.412, pred[]{:T(512)S(6)} %compare.49), kind=kOutput, calls=%fused_computation.34.clone.1.clone | convolution fusion | flops 102785024 | bytes 57345 | tf_op jit(solution)/shard_map/while/body/eval_jaxpr/dot_general | solution.py:140
  96.0 2.1 %fusion.112 = f32[8,512]{1,0:T(8,128)S(1)} fusion(f32[2048]{0:T(1024)S(1)} %bitcast.152, s32[2048]{0:T(1024)S(1)} %get-tuple-element.384, s32[2048]{0:T(1024)S(1)} %get-tuple-element.385, f32[8,512]{1,0:T(8,128)S(1)} %get-tuple-element.412, pred[]{:T(512)S(6)} %compare.49), kind=kOutput, calls=%fused_computation.34.clone.1.clone | convolution fusion | flops 102785024 | bytes 57345 | tf_op jit(solution)/shard_map/while/body/eval_jaxpr/dot_general | solution.py:140
  98.2 2.1 %fusion.112 = f32[8,512]{1,0:T(8,128)S(1)} fusion(f32[2048]{0:T(1024)S(1)} %bitcast.152, s32[2048]{0:T(1024)S(1)} %get-tuple-element.384, s32[2048]{0:T(1024)S(1)} %get-tuple-element.385, f32[8,512]{1,0:T(8,128)S(1)} %get-tuple-element.412, pred[]{:T(512)S(6)} %compare.49), kind=kOutput, calls=%fused_computation.34.clone.1.clone | convolution fusion | flops 102785024 | bytes 57345 | tf_op jit(solution)/shard_map/while/body/eval_jaxpr/dot_general | solution.py:140
  100.3 2.1 %fusion.112 = f32[8,512]{1,0:T(8,128)S(1)} fusion(f32[2048]{0:T(1024)S(1)} %bitcast.152, s32[2048]{0:T(1024)S(1)} %get-tuple-element.384, s32[2048]{0:T(1024)S(1)} %get-tuple-element.385, f32[8,512]{1,0:T(8,128)S(1)} %get-tuple-element.412, pred[]{:T(512)S(6)} %compare.49), kind=kOutput, calls=%fused_computation.34.clone.1.clone | convolution fusion | flops 102785024 | bytes 57345 | tf_op jit(solution)/shard_map/while/body/eval_jaxpr/dot_general | solution.py:140
  102.5 2.1 %fusion.112 = f32[8,512]{1,0:T(8,128)S(1)} fusion(f32[2048]{0:T(1024)S(1)} %bitcast.152, s32[2048]{0:T(1024)S(1)} %get-tuple-element.384, s32[2048]{0:T(1024)S(1)} %get-tuple-element.385, f32[8,512]{1,0:T(8,128)S(1)} %get-tuple-element.412, pred[]{:T(512)S(6)} %compare.49), kind=kOutput, calls=%fused_computation.34.clone.1.clone | convolution fusion | flops 102785024 | bytes 57345 | tf_op jit(solution)/shard_map/while/body/eval_jaxpr/dot_general | solution.py:140
  104.6 2.1 %fusion.112 = f32[8,512]{1,0:T(8,128)S(1)} fusion(f32[2048]{0:T(1024)S(1)} %bitcast.152, s32[2048]{0:T(1024)S(1)} %get-tuple-element.384, s32[2048]{0:T(1024)S(1)} %get-tuple-element.385, f32[8,512]{1,0:T(8,128)S(1)} %get-tuple-element.412, pred[]{:T(512)S(6)} %compare.49), kind=kOutput, calls=%fused_computation.34.clone.1.clone | convolution fusion | flops 102785024 | bytes 57345 | tf_op jit(solution)/shard_map/while/body/eval_jaxpr/dot_general | solution.py:140
  106.8 0.7 fusion.62
  (121 shorter events, 3.8 us)
Async XLA Ops:
  0.6 44.2 %copy-start = (bf16[1,16,128,128]{3,2,1,0:T(8,128)(2,1)S(1)}, bf16[1,16,128,128]{3,2,1,0:T(8,128)(2,1)}, u32[]{:S(2)}) copy-start(bf16[1,16,128,128]{3,2,1,0:T(8,128)(2,1)} %param.32) | copy-start | bytes 1572868
  3.1 21.9 %copy-start.11 = (s32[1,128]{1,0:T(1,128)S(1)}, s32[1,128]{1,0:T(1,128)}, u32[]{:S(2)}) copy-start(s32[1,128]{1,0:T(1,128)} %param.27) | copy-start | bytes 1540
  3.1 31.7 %copy-start.4 = (f32[2,4,512]{2,1,0:T(4,128)S(1)}, f32[2,4,512]{2,1,0:T(4,128)}, u32[]{:S(2)}) copy-start(f32[2,4,512]{2,1,0:T(4,128)} %param.23) | copy-start | bytes 49156
  3.1 36.9 %copy-start.9 = (s32[1,2,16]{2,1,0:T(2,128)S(1)}, s32[1,2,16]{2,1,0:T(2,128)}, u32[]{:S(2)}) copy-start(s32[1,2,16]{2,1,0:T(2,128)} %param.33) | copy-start | bytes 388
  3.1 36.9 %copy-start.3 = (f32[1,64,32,128]{3,2,1,0:T(8,128)S(1)}, f32[1,64,32,128]{3,2,1,0:T(8,128)}, u32[]{:S(2)}) copy-start(f32[1,64,32,128]{3,2,1,0:T(8,128)} %param.29) | copy-start | bytes 3145732
  26.5 19.5 %all-to-all-start = ((f32[16,8,128]{2,1,0:T(8,128)}), f32[16,8,128]{2,1,0:T(8,128)S(1)}, u32[]{:S(2)}, u32[]{:S(2)}) async-start(f32[16,8,128]{2,1,0:T(8,128)} %slice_bitcast_fusion.1), calls=%async_computation | async-start | bytes 131072 | tf_op jit(solution)/shard_map/all_to_all | solution.py:96
  34.9 24.4 %collective-permute-start = (f32[2,1,512]{2,1,0:T(1,128)S(1)}, f32[2,1,512]{2,1,0:T(1,128)S(1)}, u32[]{:S(2)}, u32[]{:S(2)}) collective-permute-start(f32[2,1,512]{2,1,0:T(1,128)S(1)} %get-tuple-element.290), channel_id=1, source_target_pairs={{0,2},{2,4},{4,6},{6,8},{8,10},{10,12},{12,14},{14,16},{16,18},{18... | collective-permute-start | bytes 12296 | tf_op jit(solution)/shard_map/ppermute | solution.py:20
  38.7 20.5 %collective-permute-start.1 = (f32[2,1,512]{2,1,0:T(1,128)S(1)}, f32[2,1,512]{2,1,0:T(1,128)S(1)}, u32[]{:S(2)}, u32[]{:S(2)}) collective-permute-start(f32[2,1,512]{2,1,0:T(1,128)S(1)} %get-tuple-element.291), channel_id=1, source_target_pairs={{2,0},{4,2},{6,4},{8,6},{10,8},{12,10},{14,12},{16,14},{18,16},{20... | collective-permute-start | bytes 12296 | tf_op jit(solution)/shard_map/ppermute | solution.py:21
  40.0 0.8 copy-start.10
  40.7 4.7 %copy-start.6 = (f32[4,32,32]{2,1,0:T(8,128)S(1)}, f32[4,32,32]{2,1,0:T(8,128)}, u32[]{:S(2)}) copy-start(f32[4,32,32]{2,1,0:T(8,128)} %param.31) | copy-start | bytes 49156
  40.7 4.7 %copy-start.8 = (s32[1,64]{1,0:T(1,128)S(1)}, s32[1,64]{1,0:T(1,128)}, u32[]{:S(2)}) copy-start(s32[1,64]{1,0:T(1,128)} %param.30) | copy-start | bytes 772
  46.0 15.2 %all-to-all-start.1 = ((f32[16,8,128]{2,1,0:T(8,128)}), f32[16,8,128]{2,1,0:T(8,128)S(1)}, u32[]{:S(2)}, u32[]{:S(2)}) async-start(f32[16,8,128]{2,1,0:T(8,128)} %slice_bitcast_fusion), calls=%async_computation.1 | async-start | bytes 131072 | tf_op jit(solution)/shard_map/all_to_all | solution.py:95
  66.8 1.0 copy-start.1
  73.4 1.0 copy-start.2
  75.7 13.1 %all-to-all-start.2 = ((f32[16,8,128]{2,1,0:T(8,128)}), f32[16,8,128]{2,1,0:T(8,128)S(1)}, u32[]{:S(2)}, u32[]{:S(2)}) async-start(f32[16,8,128]{2,1,0:T(8,128)} %bitcast.38), calls=%async_computation.2 | async-start | bytes 131072 | tf_op jit(solution)/shard_map/all_to_all | solution.py:131
  81.2 25.5 %collective-permute-start.2 = (f32[1,6,512]{2,1,0:T(8,128)S(1)}, f32[1,6,512]{2,1,0:T(8,128)S(1)}, u32[]{:S(2)}, u32[]{:S(2)}) collective-permute-start(f32[1,6,512]{2,1,0:T(8,128)S(1)} %get-tuple-element.284), channel_id=1, source_target_pairs={{0,1},{2,3},{4,5},{6,7},{8,9},{10,11},{12,13},{14,15},{16,17},{18,... | collective-permute-start | bytes 36872 | tf_op jit(solution)/shard_map/ppermute | solution.py:20
  83.2 23.5 %collective-permute-start.3 = (f32[1,6,512]{2,1,0:T(8,128)S(1)}, f32[1,6,512]{2,1,0:T(8,128)S(1)}, u32[]{:S(2)}, u32[]{:S(2)}) collective-permute-start(f32[1,6,512]{2,1,0:T(8,128)S(1)} %get-tuple-element.285), channel_id=1, source_target_pairs={{1,0},{3,2},{5,4},{7,6},{9,8},{11,10},{13,12},{15,14},{17,16},{19,... | collective-permute-start | bytes 36872 | tf_op jit(solution)/shard_map/ppermute | solution.py:21
  89.5 17.2 %copy-start.5 = (f32[3,2,4,512]{3,2,1,0:T(4,128)S(1)}, f32[3,2,4,512]{3,2,1,0:T(4,128)}, u32[]{:S(2)}) copy-start(f32[3,2,4,512]{3,2,1,0:T(4,128)} %param.24) | copy-start | bytes 147460
  89.5 17.2 %copy-start.7 = (f32[2,4,512]{2,1,0:T(4,128)S(1)}, f32[2,4,512]{2,1,0:T(4,128)}, u32[]{:S(2)}) copy-start(f32[2,4,512]{2,1,0:T(4,128)} %param.25) | copy-start | bytes 49156
where the time goes:
time: 108 us; the launch traced here: 107 us
  matrix products  42.9 us (40%)
  starting transfers between devices  29.8 us (28%)
  local copies, waits for them, and re-layouts  17.7 us (16%)
  waiting for transfers between devices  5.66 us (5%)
  blocking collectives  5.23 us (5%)
  other arithmetic  4.28 us (4%)
  between operations  1.18 us (1%)
    dot_general x8, matrix products, lookup(): lax.dot_general(column_hot, both_lines, (((1,), (1,)), ((), ())), precisi...  17.5 us
    dot_general x8, matrix products, deposit(): lax.dot_general(line_hot, weighted, (((0,), (0,)), ((), ())), precision=l...  16.6 us
    all_to_all x1, starting transfers between devices, on_device(): lax.all_to_all(coef_out, 'xy', split_axis=0, concat_axis=0, tiled=True)  8.31 us
    all_to_all x1, starting transfers between devices, on_device(): lax.all_to_all(air_out, 'xy', split_axis=0, concat_axis=0, tiled=True)  7.64 us
    dot_general x4, matrix products, on_device(): jnp.einsum('tab,tbf->taf', inverse_tile, temps, precision=lax.Precision.H...  7.61 us
    ppermute x2, starting transfers between devices, with_halo(): before = lax.ppermute(last, axis, up)  5.79 us
    all_to_all x1, starting transfers between devices, on_device(): lax.all_to_all(back_rows, 'xy', split_axis=0, concat_axis=0, tiled=True)  5.51 us
    all_to_all x1, waiting for transfers between devices, on_device(): lax.all_to_all(back_rows, 'xy', split_axis=0, concat_axis=0, tiled=True)  4.25 us
  transfers between devices with their start and end apart: 7, of which 2 were waited for; matrix products, arithmetic and copies ran while one was open for 23% of the time, Pallas kernels for 0%

commit v1 on v0

v1 whole, which is shorter than its diff:
```python
import jax
import jax.numpy as jnp
from jax import lax
from jax.experimental import pallas as pl
from jax.experimental.pallas import tpu as pltpu
from jax.sharding import PartitionSpec as P

SUB = 4


wall_gain = 0.25
flux_gain = 0.5


def upwind(speed, centre, lower, upper):
    return jnp.maximum(speed, 0.0) * (centre - lower) + jnp.minimum(speed, 0.0) * (upper - centre)


LANES = 128
HIGH = lax.Precision.HIGHEST
VMEM_LIMIT = 40 * 1024 * 1024


def contract(a, b, dims):
    return lax.dot_general(
        a, b, (dims, ((), ())), precision=HIGH, preferred_element_type=jnp.float32
    )


def slot_matrix(send_ref, total):
    slots = send_ref.shape[1]
    row_ids = lax.broadcasted_iota(jnp.int32, (total, slots), 0)
    return (row_ids == send_ref[...]).astype(jnp.float32)


def lookup_kernel(theta_ref, wind_ref, cell_ref, send_ref, out_ref, coef_ref, found_ref):
    levels, rows, y_cells = theta_ref.shape
    slots, width = found_ref.shape[0], found_ref.shape[1] // 2
    pieces = y_cells // LANES
    w0, w1, w2 = wind_ref[0], wind_ref[1], wind_ref[2]
    coef_ref[...] = 0.5 + 4.0 * (w0 * w0 + w1 * w1 + w2 * w2)

    def group(g, carry):
        start = pl.multiple_of(g * 8, 8)
        cells = cell_ref[0, pl.ds(start, 8), :]
        lane = cells % LANES
        piece = cells // LANES
        air = jnp.zeros((8, width), jnp.float32)
        coef = jnp.zeros((8, width), jnp.float32)
        for b in range(levels * rows * pieces):
            line, j = b // pieces, b % pieces
            z, x = line // rows, line % rows
            cut = slice(j * LANES, (j + 1) * LANES)
            hit = piece == b
            theta_row = jnp.broadcast_to(theta_ref[z, x : x + 1, cut], (8, LANES))
            coef_row = jnp.broadcast_to(coef_ref[z, x : x + 1, cut], (8, LANES))
            air = jnp.where(hit, jnp.take_along_axis(theta_row, lane, axis=1), air)
            coef = jnp.where(hit, jnp.take_along_axis(coef_row, lane, axis=1), coef)
        found_ref[pl.ds(start, 8), :width] = air
        found_ref[pl.ds(start, 8), width:] = coef
        return carry

    lax.fori_loop(0, slots // 8, group, 0)
    count, capacity = out_ref.shape[0], out_ref.shape[1]
    listed = contract(slot_matrix(send_ref, count * capacity), found_ref[...], ((1,), (0,)))
    for j in range(count):
        out_ref[j] = listed[j * capacity : (j + 1) * capacity]


def heat_kernel(
    theta_ref, wind_ref, eddy_ref, cell_ref, send_ref, back_ref,
    low_x_ref, high_x_ref, low_z_ref, high_z_ref, out_ref, rows_ref, flux_ref,
):
    levels, rows, y_cells = theta_ref.shape
    lines, pieces = levels * rows, y_cells // LANES
    slots, width = flux_ref.shape
    count, capacity = back_ref.shape[0], back_ref.shape[1]
    for j in range(count):
        rows_ref[j * capacity : (j + 1) * capacity, :] = back_ref[j]
    flux_ref[...] = contract(
        slot_matrix(send_ref, count * capacity), rows_ref[...], ((0,), (0,))
    )
    step = 8
    row_ids = lax.broadcasted_iota(jnp.int32, (lines * pieces, width), 0)
    lane_ids = lax.broadcasted_iota(jnp.int32, (LANES, width), 0)

    def group(g, total):
        start = pl.multiple_of(g * step, step)
        cells = cell_ref[0, pl.ds(start, step), :]
        flux = flux_ref[pl.ds(start, step), :]
        lane = cells % LANES
        place = (cells % y_cells) // LANES * lines + cells // y_cells
        upper = flux.astype(jnp.bfloat16).astype(jnp.float32)
        lower = flux - upper
        left, right = [], []
        for s in range(step):
            hit = row_ids == place[s : s + 1]
            left.append(
                jnp.concatenate(
                    (jnp.where(hit, upper[s : s + 1], 0.0), jnp.where(hit, lower[s : s + 1], 0.0)), 0
                ).astype(jnp.bfloat16)
            )
            right.append(
                jnp.where(lane_ids == lane[s : s + 1], 1.0, 0.0).astype(jnp.bfloat16)
            )
        return total + lax.dot_general(
            jnp.concatenate(left, 1),
            jnp.concatenate(right, 1),
            (((1,), (1,)), ((), ())),
            preferred_element_type=jnp.float32,
        )

    total = lax.fori_loop(
        0, slots // step, group, jnp.zeros((2 * lines * pieces, LANES), jnp.float32)
    )
    total = total[: lines * pieces] + total[lines * pieces :]
    heat = jnp.concatenate([total[j * lines : (j + 1) * lines] for j in range(pieces)], 1)
    for z in range(levels):
        c = theta_ref[z]
        lower_z = low_z_ref[...] if z == 0 else theta_ref[z - 1]
        upper_z = high_z_ref[...] if z == levels - 1 else theta_ref[z + 1]
        lower_x = jnp.concatenate((low_x_ref[z : z + 1], c[:-1]), 0)
        upper_x = jnp.concatenate((c[1:], high_x_ref[z : z + 1]), 0)
        lower_y = jnp.roll(c, 1, axis=1)
        upper_y = jnp.roll(c, -1, axis=1)
        advect = (
            upwind(wind_ref[0, z], c, lower_z, upper_z)
            + upwind(wind_ref[1, z], c, lower_x, upper_x)
            + upwind(wind_ref[2, z], c, lower_y, upper_y)
        )
        laplace = lower_z + upper_z + lower_x + upper_x + lower_y + upper_y - 6.0 * c
        out_ref[z] = (
            c - advect + eddy_ref[z] * laplace + flux_gain * heat[z * rows : (z + 1) * rows]
        )


def call_lookup(theta, wind, cells, send, count, capacity):
    slots, width = cells.shape[1], cells.shape[2]
    return pl.pallas_call(
        lookup_kernel,
        out_shape=jax.ShapeDtypeStruct((count, capacity, 2 * width), jnp.float32),
        in_specs=[pl.BlockSpec(memory_space=pltpu.VMEM)] * 4,
        out_specs=pl.BlockSpec(memory_space=pltpu.VMEM),
        scratch_shapes=[
            pltpu.VMEM(theta.shape, jnp.float32),
            pltpu.VMEM((slots, 2 * width), jnp.float32),
        ],
        compiler_params=pltpu.CompilerParams(vmem_limit_bytes=VMEM_LIMIT),
        name="lookup",
    )(theta, wind, cells, send)


def call_heat(theta, wind, eddy, cells, send, back, halos):
    slots, width = cells.shape[1], cells.shape[2]
    return pl.pallas_call(
        heat_kernel,
        out_shape=jax.ShapeDtypeStruct(theta.shape, jnp.float32),
        in_specs=[pl.BlockSpec(memory_space=pltpu.VMEM)] * 10,
        out_specs=pl.BlockSpec(memory_space=pltpu.VMEM),
        scratch_shapes=[
            pltpu.VMEM((back.shape[0] * back.shape[1], width), jnp.float32),
            pltpu.VMEM((slots, width), jnp.float32),
        ],
        compiler_params=pltpu.CompilerParams(vmem_limit_bytes=VMEM_LIMIT),
        name="heat",
    )(theta, wind, eddy, cells, send, back, *halos)


def on_device(
    potential_temp,
    wind_field,
    eddy_diff,
    facade_cell,
    tile_send,
    tile_take,
    wall_temp,
    wall_class,
    wall_inverse,
    refl_block,
    refl_pair,
):
    levels, x_rows, y_cells = potential_temp.shape
    tile_slots = facade_cell.shape[1]
    tile_width = facade_cell.shape[2]
    owned = tile_take.shape[1]
    node_count = wall_temp.shape[2]
    xy_count = lax.axis_size("xy")
    capacity = 2 * owned // xy_count
    slot_total = xy_count * capacity
    listed = call_lookup(potential_temp, wind_field, facade_cell, tile_send, xy_count, capacity)
    halos = []
    for axis, dim in (("xy", 1), ("gz", 0)):
        size, length = lax.axis_size(axis), potential_temp.shape[dim]
        up = [(i, i + 1) for i in range(size - 1)]
        down = [(j, i) for i, j in up]
        halos.append(lax.ppermute(lax.index_in_dim(potential_temp, length - 1, dim, False), axis, up))
        halos.append(lax.ppermute(lax.index_in_dim(potential_temp, 0, dim, False), axis, down))
    received = lax.all_to_all(listed, "xy", split_axis=0, concat_axis=0, tiled=True)
    received = received.reshape(slot_total, 2 * tile_width)
    take_rows = tile_take.reshape(owned)
    own_both = received[take_rows]
    own_air, own_coef = own_both[:, :tile_width], own_both[:, tile_width:]
    wall_state = wall_temp.reshape(owned, node_count, tile_width)
    emitted = wall_state[:, 0, :].astype(jnp.bfloat16)
    district = lax.all_gather(emitted, "gz", axis=0, tiled=True)
    blocks = refl_block[0]
    pair_rows = refl_pair[0]
    source_emit = district[pair_rows[1]]
    contrib = jnp.einsum("bij,bj->bi", blocks, source_emit, preferred_element_type=jnp.float32)
    targets = pair_rows[0]
    district_rows = lax.axis_size("gz") * owned
    row_ids = lax.iota(jnp.int32, district_rows)
    one_hot = (row_ids[:, None] == targets[None, :]).astype(jnp.float32)
    whole = lax.psum(
        jnp.dot(
            one_hot, contrib, precision=lax.Precision.HIGHEST, preferred_element_type=jnp.float32
        ).astype(jnp.bfloat16),
        "gz",
    ).astype(jnp.float32)
    own_rad = lax.dynamic_slice_in_dim(whole, lax.axis_index("gz") * owned, owned, 0)
    class_ids = lax.broadcasted_iota(jnp.int32, (owned, wall_inverse.shape[0]), 1)
    class_hot = (wall_class.reshape(owned)[:, None] == class_ids).astype(jnp.float32)
    inverse_tile = jnp.einsum(
        "tc,cab->tab", class_hot, wall_inverse, precision=lax.Precision.HIGHEST
    )
    temps = wall_state
    for substep in range(SUB):
        forcing = own_coef * (own_air - temps[:, 0, :]) + own_rad
        temps = temps.at[:, 0, :].add(wall_gain * forcing)
        temps = jnp.einsum("tab,tbf->taf", inverse_tile, temps, precision=lax.Precision.HIGHEST)
    flux_out = own_coef * (temps[:, 0, :] - own_air)
    back_rows = jnp.zeros((slot_total, tile_width), jnp.float32).at[take_rows].set(flux_out)
    returned = lax.all_to_all(
        back_rows.reshape(xy_count, capacity, tile_width), "xy", split_axis=0, concat_axis=0, tiled=True
    )
    temp_next = call_heat(
        potential_temp, wind_field, eddy_diff, facade_cell, tile_send, returned, halos
    )
    return (temp_next, temps.reshape(1, owned, node_count, tile_width))


def solution(mesh):
    in_specs = (
        P("gz", "xy", None),
        P(None, "gz", "xy", None),
        P("gz", "xy", None),
        P("gz", "xy", None),
        P("gz", "xy"),
        P("gz", "xy"),
        P("gz", "xy", None, None),
        P("gz", "xy"),
        P(),
        P("xy", "gz", None, None),
        P("xy", None, "gz"),
    )
    out_specs = (P("gz", "xy", None), P("gz", "xy", None, None))
    return jax.shard_map(
        on_device, mesh=mesh, in_specs=in_specs, out_specs=out_specs, check_vma=False
    )
```

time: 108 us -> 67.3 us (0.62)
  matrix products: 42.9 us -> 8.78 us
  Pallas kernels: 0 us -> 7.75 us
  starting transfers between devices: 29.8 us -> 23.2 us
  local copies, waits for them, and re-layouts: 17.7 us -> 12.9 us
  other arithmetic: 4.28 us -> 2.03 us
  waiting for transfers between devices: 5.66 us -> 4.2 us
  blocking collectives: 5.23 us -> 6.32 us
    dot_general x16 -> x0, matrix products: 34.1 us -> none  [the longest x8 17.5 us: lookup(): lax.dot_general(column_hot, both_lines, (((1,), (1,)), ((), ())), precisi...]
    pallas_call x0 -> x2, Pallas kernels: none -> 7.75 us  [the longest x1 4.51 us: call_heat(): pl.pallas_call(heat_kernel, out_shape=jax.ShapeDtypeStruct(theta.shape, j...]
    all_to_all x3 -> x2, starting transfers between devices: 21.5 us -> 15.3 us  [the longest x1 8.44 us: on_device(): lax.all_to_all(listed, 'xy', split_axis=0, concat_axis=0, tiled=True)]
    all_to_all x3 -> x2, waiting for transfers between devices: 5.64 us -> 0.01 us  [the longest x1 0.01 us: on_device(): lax.all_to_all(listed, 'xy', split_axis=0, concat_axis=0, tiled=True)]
    unnamed x26 -> x36, local copies, waits for them, and re-layouts: 3.58 us -> 8.5 us
    ppermute x4, waiting for transfers between devices: 0.01 us -> 4.2 us  [the longest x2 4.19 us: on_device(): lax.ppermute(lax.index_in_dim(potential_temp, 0, dim, False), axis, down)]
    dynamic_update_slice x16 -> x0, local copies, waits for them, and re-layouts: 3.25 us -> none  [on_device(): theta_found, speed_found = lax.map(lookup, index_blocks)]
    scatter x2 -> x0, local copies, waits for them, and re-layouts: 1.72 us -> none  [the longest x1 0.86 us: on_device(): coef_out = empty_box.at[target_rows].set(coef_slots)[:slot_total]]
  transfers between devices with their start and end apart: 7 -> 6, of which waited for: 2 -> 1; matrix products, arithmetic and copies ran while one was open for 23% -> 27% of each run, Pallas kernels for 0% -> 0%
where the time goes in v1:
time: 67.3 us; the launch traced here: 66.2 us
  starting transfers between devices  23.2 us (34%)
  local copies, waits for them, and re-layouts  12.9 us (19%)
  matrix products  8.78 us (13%)
  Pallas kernels  7.75 us (12%)
  blocking collectives  6.32 us (9%)
  waiting for transfers between devices  4.2 us (6%)
  other arithmetic  2.03 us (3%)
  between operations  1.05 us (2%)
    unnamed x36, local copies, waits for them, and re-layouts  8.5 us
    all_to_all x1, starting transfers between devices, on_device(): lax.all_to_all(listed, 'xy', split_axis=0, concat_axis=0, tiled=True)  8.44 us
    dot_general x4, matrix products, on_device(): jnp.einsum('tab,tbf->taf', inverse_tile, temps, precision=lax.Precision.H...  7.61 us
    all_to_all x1, starting transfers between devices, on_device(): lax.all_to_all(back_rows.reshape(xy_count, capacity, tile_width), 'xy', s...  6.87 us
    ppermute x2, starting transfers between devices, on_device(): lax.ppermute(lax.index_in_dim(potential_temp, length - 1, dim, False), ax...  5.28 us
    pallas_call x1, Pallas kernels, call_heat(): pl.pallas_call(heat_kernel, out_shape=jax.ShapeDtypeStruct(theta.shape, j...  4.51 us
    ppermute x2, waiting for transfers between devices, on_device(): lax.ppermute(lax.index_in_dim(potential_temp, 0, dim, False), axis, down)  4.19 us
    psum x1, blocking collectives, on_device(): lax.psum(jnp.dot(one_hot, contrib, precision=lax.Precision.HIGHEST, prefe...  3.58 us
  transfers between devices with their start and end apart: 6, of which 1 were waited for; matrix products, arithmetic and copies ran while one was open for 27% of the time, Pallas kernels for 0%

profile of v1, /device:TPU:0, one launch (start us, length us, event | category | flops | bytes accessed | tf_op | source)
XLA Modules:
  0.0 66.2 jit_solution(2970291986207228318)
XLA Ops:
  0.6 0.0 copy-start
  0.6 0.0 copy-start.1
  0.7 0.9 %copy-done.1 = s32[1,128,128]{2,1,0:T(8,128)S(1)} copy-done((s32[1,128,128]{2,1,0:T(8,128)S(1)}, s32[1,128,128]{2,1,0:T(8,128)}, u32[]{:S(2)}) %copy-start.1) | copy-done | bytes 65560
  1.5 0.7 %copy-done.3 = f32[2,4,512]{2,1,0:T(4,128)S(1)} copy-done((f32[2,4,512]{2,1,0:T(4,128)S(1)}, f32[2,4,512]{2,1,0:T(4,128)}, u32[]{:S(2)}) %copy-start.3) | copy-done | bytes 16408
  2.3 0.0 copy-start.5
  2.3 0.8 %copy-done.5 = f32[3,2,4,512]{3,2,1,0:T(4,128)S(1)} copy-done((f32[3,2,4,512]{3,2,1,0:T(4,128)S(1)}, f32[3,2,4,512]{3,2,1,0:T(4,128)}, u32[]{:S(2)}) %copy-start.5) | copy-done | bytes 49176
  3.1 0.0 copy-start.8
  3.1 0.7 copy-done.8
  3.7 3.2 %lookup.1 = f32[16,8,256]{2,1,0:T(8,128)} custom-call(f32[2,4,512]{2,1,0:T(4,128)S(1)} %copy-done.3, f32[3,2,4,512]{3,2,1,0:T(4,128)S(1)} %copy-done.5, s32[1,128,128]{2,1,0:T(8,128)S(1)} %copy-done.1, s32[1,128]{1,0:T(1,128)S(1)} %copy-done.8), custom_call_target="tpu_custom_call" | custom-call | tf_op jit(solution)/shard_map/lookup/pallas_call | solution.py:139
  7.0 0.0 copy-start.4
  7.0 8.4 %all-to-all-start = ((f32[16,8,256]{2,1,0:T(8,128)}), f32[16,8,256]{2,1,0:T(8,128)S(1)}, u32[]{:S(2)}, u32[]{:S(2)}) async-start(f32[16,8,256]{2,1,0:T(8,128)} %lookup.1), calls=%async_computation | async-start | bytes 262144 | tf_op jit(solution)/shard_map/all_to_all | solution.py:198
  15.4 0.0 copy-done.4
  15.4 1.5 %collective-permute-start.2 = (f32[4,512]{1,0:T(4,128)S(1)}, f32[4,512]{1,0:T(4,128)S(1)}, u32[]{:S(2)}, u32[]{:S(2)}) collective-permute-start(f32[4,512]{1,0:T(4,128)S(1)} %get-tuple-element.53), channel_id=1, source_target_pairs={{0,1},{2,3},{4,5},{6,7},{8,9},{10,11},{12,13},{14,15},{16,17},{18,... | collective-permute-start | bytes 24584 | tf_op jit(solution)/shard_map/ppermute | solution.py:196
  16.9 0.0 copy-start.14
  16.9 1.3 %collective-permute-start.3 = (f32[4,512]{1,0:T(4,128)S(1)}, f32[4,512]{1,0:T(4,128)S(1)}, u32[]{:S(2)}, u32[]{:S(2)}) collective-permute-start(f32[4,512]{1,0:T(4,128)S(1)} %get-tuple-element.52), channel_id=1, source_target_pairs={{1,0},{3,2},{5,4},{7,6},{9,8},{11,10},{13,12},{15,14},{17,16},{19,... | collective-permute-start | bytes 24584 | tf_op jit(solution)/shard_map/ppermute | solution.py:197
  18.2 0.0 copy-done.14
  18.3 1.8 %copy.50 = f32[1,64,32,128]{3,1,2,0:T(8,128)S(1)} copy(f32[1,64,32,128]{3,2,1,0:T(8,128)} %param.25) | data formatting | bytes 2097152 | tf_op args[6]
  20.1 0.0 copy-start.15
  20.1 1.0 %copy.51 = f32[64,32,128]{2,0,1:T(8,128)} copy(f32[64,32,128]{2,0,1:T(8,128)S(1)} %bitcast.83) | data formatting | bytes 2097152
  21.1 0.0 copy-start.12
  21.1 2.7 %all_gather.3 = bf16[128,128]{1,0:T(8,128)(2,1)S(1)} all-gather(bf16[64,128]{1,0:T(8,128)(2,1)S(1)} %fusion.24), channel_id=1, replica_groups=mesh['xy'=16,'gz'=2] {'gz'}, dimensions={0}, use_global_device_ids=true | all-gather | bytes 49152 | tf_op jit(solution)/shard_map/all_gather | solution.py:205
  23.8 0.0 copy-done.15
  23.9 0.0 copy-start.13
  23.9 0.0 copy-done.12
  23.9 0.6 copy-done.13
  24.5 0.6 fusion.4
  25.1 0.9 %copy.26 = f32[64,32,32]{2,1,0:T(8,128)S(1)} copy(f32[64,32,32]{0,2,1:T(8,128)S(1)} %fusion.4) | data formatting | bytes 524288 | tf_op jit(solution)/shard_map/tc,cab->tab/dot_general | solution.py:223
  26.1 0.6 gather_fusion.1
  26.7 0.0 copy-done
  26.7 0.4 fusion.2
  27.0 0.2 convolution_convert_fusion
  27.2 3.6 %psum.7 = bf16[128,128]{1,0:T(8,128)(2,1)S(1)} all-reduce(bf16[128,128]{1,0:T(8,128)(2,1)S(1)} %convolution_convert_fusion), channel_id=1, replica_groups=mesh['xy'=16,'gz'=2] {'gz'}, use_global_device_ids=true, to_apply=%region_0.0 | all-reduce | flops 16384 | bytes 65536 | tf_op jit(solution)/shard_map/psum | solution.py:214
  30.8 0.0 all-to-all-done
  30.8 0.7 gather_fusion
  31.5 0.6 fusion.12
  32.1 2.9 %fusion = f32[64,32,128]{2,1,0:T(8,128)S(1)} fusion(f32[64,32,32]{2,1,0:T(8,128)S(1)} %copy.26, f32[64,32,128]{2,0,1:T(8,128)} %fusion.12), kind=kOutput, calls=%fused_computation.4 | convolution fusion | flops 100663296 | bytes 2359296 | tf_op jit(solution)/shard_map/tab,tbf->taf/dot_general | solution.py:230
  35.1 0.2 scatter-add.15
  35.3 1.2 %fusion.35 = f32[64,32,128]{2,1,0:T(8,128)S(1)} fusion(f32[64,32,32]{2,1,0:T(8,128)S(1)} %copy.26, f32[64,32,128]{2,1,0:T(8,128)S(1)} %scatter-add.15), kind=kOutput, calls=%fused_computation.56 | convolution fusion | flops 100663296 | bytes 2359296 | tf_op jit(solution)/shard_map/tab,tbf->taf/dot_general | solution.py:230
  36.5 0.0 copy-start.10
  36.5 1.0 %copy-done.10 = f32[64,32,128]{2,1,0:T(8,128)} copy-done((f32[64,32,128]{2,1,0:T(8,128)}, f32[64,32,128]{2,1,0:T(8,128)S(1)}, u32[]{:S(2)}) %copy-start.10) | copy-done | bytes 1048600
  37.5 1.7 %scatter-add.16 = f32[64,32,128]{2,1,0:T(8,128)} dynamic-update-slice(f32[64,32,128]{2,1,0:T(8,128)} %copy-done.10, f32[64,1,128]{2,1,0:T(1,128)S(1)} %bitcast.96, s32[]{:T(128)} %constant.100.clone.1, s32[]{:T(128)} %constant.100.clone.1, s32[]{:T(128)} %constant.100.clone.1) | dynamic-update-slice | bytes 65540 | tf_op jit(solution)/shard_map/scatter-add | solution.py:229
  39.3 2.4 %fusion.36 = f32[64,32,128]{2,1,0:T(8,128)S(1)} fusion(f32[64,32,32]{2,1,0:T(8,128)S(1)} %copy.26, f32[64,32,128]{2,1,0:T(8,128)} %scatter-add.16), kind=kOutput, calls=%fused_computation.57 | convolution fusion | flops 100663296 | bytes 2359296 | tf_op jit(solution)/shard_map/tab,tbf->taf/dot_general | solution.py:230
  41.7 0.2 scatter-add.19
  41.9 1.2 %fusion.37 = f32[64,32,128]{2,1,0:T(8,128)S(1)} fusion(f32[64,32,32]{2,1,0:T(8,128)S(1)} %copy.26, f32[64,32,128]{2,1,0:T(8,128)S(1)} %scatter-add.19), kind=kOutput, calls=%fused_computation.58 | convolution fusion | flops 100663296 | bytes 2359296 | tf_op jit(solution)/shard_map/tab,tbf->taf/dot_general | solution.py:230
  43.0 0.0 copy-start.11
  43.1 1.0 %copy-done.11 = f32[64,32,128]{2,1,0:T(8,128)} copy-done((f32[64,32,128]{2,1,0:T(8,128)}, f32[64,32,128]{2,1,0:T(8,128)S(1)}, u32[]{:S(2)}) %copy-start.11) | copy-done | bytes 1048600
  44.1 1.3 %scatter_custom_fusion = f32[128,128]{1,0:T(8,128)} fusion(s32[64]{0:T(128)S(1)} %fusion.31, f32[64,128]{1,0:T(8,128)S(1)} %bitcast.93, f32[]{:T(128)} %constant.99.clone.1, f32[64,256]{1,0:T(8,128)S(1)} %gather_fusion), kind=kCustom, calls=%fused_computation.30 | custom fusion | flops 16384 | bytes 163844 | tf_op jit(solution)/shard_map/scatter | solution.py:232
  45.4 0.0 copy-start.2
  45.4 0.0 copy-start.6
  45.4 6.9 %all-to-all-start.1 = ((f32[16,8,128]{2,1,0:T(8,128)}), f32[16,8,128]{2,1,0:T(8,128)S(1)}, u32[]{:S(2)}, u32[]{:S(2)}) async-start(f32[16,8,128]{2,1,0:T(8,128)} %bitcast.26), calls=%async_computation.1 | async-start | bytes 131072 | tf_op jit(solution)/shard_map/all_to_all | solution.py:233
  52.3 0.0 copy-start.7
  52.3 3.8 %collective-permute-start = (f32[2,512]{1,0:T(2,128)S(1)}, f32[2,512]{1,0:T(2,128)S(1)}, u32[]{:S(2)}, u32[]{:S(2)}) collective-permute-start(f32[2,512]{1,0:T(2,128)S(1)} %bitcast.99), channel_id=1, source_target_pairs={{0,2},{2,4},{4,6},{6,8},{8,10},{10,12},{12,14},{14,16},{16,18},{18... | collective-permute-start | bytes 12296 | tf_op jit(solution)/shard_map/ppermute | solution.py:196
  56.1 0.0 copy-start.9
  56.2 1.3 %collective-permute-start.1 = (f32[2,512]{1,0:T(2,128)S(1)}, f32[2,512]{1,0:T(2,128)S(1)}, u32[]{:S(2)}, u32[]{:S(2)}) collective-permute-start(f32[2,512]{1,0:T(2,128)S(1)} %bitcast.100), channel_id=1, source_target_pairs={{2,0},{4,2},{6,4},{8,6},{10,8},{12,10},{14,12},{16,14},{18,16},{20... | collective-permute-start | bytes 12296 | tf_op jit(solution)/shard_map/ppermute | solution.py:197
  57.5 0.0 collective-permute-done.low_x_ref
  57.5 4.2 %collective-permute-done.1.high_x_ref = f32[2,512]{1,0:T(2,128)S(1)} collective-permute-done((f32[2,512]{1,0:T(2,128)S(1)}, f32[2,512]{1,0:T(2,128)S(1)}, u32[]{:S(2)}, u32[]{:S(2)}) %collective-permute-start.1) | collective-permute-done | bytes 4128 | tf_op jit(solution)/shard_map/ppermute | solution.py:197
  61.7 0.0 collective-permute-done.2.low_z_ref
  61.7 0.0 collective-permute-done.3.high_z_ref
  61.7 0.0 all-to-all-done.1.back_ref
  61.7 0.0 copy-done.2
  61.7 0.0 copy-done.6
  61.7 0.0 copy-done.7
  61.7 0.0 copy-done.9
  61.7 4.5 %heat.1 = f32[2,4,512]{2,1,0:T(4,128)} custom-call(f32[2,4,512]{2,1,0:T(4,128)S(1)} %copy-done.4, f32[3,2,4,512]{3,2,1,0:T(4,128)S(1)} %copy-done.6, f32[2,4,512]{2,1,0:T(4,128)S(1)} %copy-done.7, s32[1,128,128]{2,1,0:T(8,128)S(1)} %copy-done.2, s32[1,128]{1,0:T(1,128)S(1)} %copy-done.9, f32[16,8,128]{2,1,0:T(8,128)S(1)} %all-to-all-done.1.back_ref, ...), custom_call_target="tpu_custom_call" | custom-call | tf_op jit(solution)/shard_map/heat/pallas_call | solution.py:155
  (19 shorter events, 0.2 us)
Async XLA Ops:
  0.6 26.0 %copy-start = (bf16[1,16,128,128]{3,2,1,0:T(8,128)(2,1)S(1)}, bf16[1,16,128,128]{3,2,1,0:T(8,128)(2,1)}, u32[]{:S(2)}) copy-start(bf16[1,16,128,128]{3,2,1,0:T(8,128)(2,1)} %param.28) | copy-start | bytes 1572868
  0.6 0.9 %copy-start.1 = (s32[1,128,128]{2,1,0:T(8,128)S(1)}, s32[1,128,128]{2,1,0:T(8,128)}, u32[]{:S(2)}) copy-start(s32[1,128,128]{2,1,0:T(8,128)} %cell_ref.3) | copy-start | bytes 196612
  1.5 0.7 %copy-start.3 = (f32[2,4,512]{2,1,0:T(4,128)S(1)}, f32[2,4,512]{2,1,0:T(4,128)}, u32[]{:S(2)}) copy-start(f32[2,4,512]{2,1,0:T(4,128)} %theta_ref.3) | copy-start | bytes 49156
  2.3 0.8 %copy-start.5 = (f32[3,2,4,512]{3,2,1,0:T(4,128)S(1)}, f32[3,2,4,512]{3,2,1,0:T(4,128)}, u32[]{:S(2)}) copy-start(f32[3,2,4,512]{3,2,1,0:T(4,128)} %wind_ref.3) | copy-start | bytes 147460
  3.1 0.7 copy-start.8
  7.0 8.5 %copy-start.4 = (f32[2,4,512]{2,1,0:T(4,128)S(1)}, f32[2,4,512]{2,1,0:T(4,128)}, u32[]{:S(2)}) copy-start(f32[2,4,512]{2,1,0:T(4,128)} %theta_ref.3) | copy-start | bytes 49156
  7.0 23.9 %all-to-all-start = ((f32[16,8,256]{2,1,0:T(8,128)}), f32[16,8,256]{2,1,0:T(8,128)S(1)}, u32[]{:S(2)}, u32[]{:S(2)}) async-start(f32[16,8,256]{2,1,0:T(8,128)} %lookup.1), calls=%async_computation | async-start | bytes 262144 | tf_op jit(solution)/shard_map/all_to_all | solution.py:198
  15.4 46.2 %collective-permute-start.2 = (f32[4,512]{1,0:T(4,128)S(1)}, f32[4,512]{1,0:T(4,128)S(1)}, u32[]{:S(2)}, u32[]{:S(2)}) collective-permute-start(f32[4,512]{1,0:T(4,128)S(1)} %get-tuple-element.53), channel_id=1, source_target_pairs={{0,1},{2,3},{4,5},{6,7},{8,9},{10,11},{12,13},{14,15},{16,17},{18,... | collective-permute-start | bytes 24584 | tf_op jit(solution)/shard_map/ppermute | solution.py:196
  16.9 1.3 %copy-start.14 = (s32[1,2,16]{2,1,0:T(2,128)S(1)}, s32[1,2,16]{2,1,0:T(2,128)}, u32[]{:S(2)}) copy-start(s32[1,2,16]{2,1,0:T(2,128)} %param.29) | copy-start | bytes 388
  16.9 44.7 %collective-permute-start.3 = (f32[4,512]{1,0:T(4,128)S(1)}, f32[4,512]{1,0:T(4,128)S(1)}, u32[]{:S(2)}, u32[]{:S(2)}) collective-permute-start(f32[4,512]{1,0:T(4,128)S(1)} %get-tuple-element.52), channel_id=1, source_target_pairs={{1,0},{3,2},{5,4},{7,6},{9,8},{11,10},{13,12},{15,14},{17,16},{19,... | collective-permute-start | bytes 24584 | tf_op jit(solution)/shard_map/ppermute | solution.py:197
  20.1 3.7 %copy-start.15 = (s32[1,64]{1,0:T(1,128)S(1)}, s32[1,64]{1,0:T(1,128)}, u32[]{:S(2)}) copy-start(s32[1,64]{1,0:T(1,128)} %param.24) | copy-start | bytes 772
  21.1 2.8 %copy-start.12 = (f32[4,32,32]{2,1,0:T(8,128)S(1)}, f32[4,32,32]{2,1,0:T(8,128)}, u32[]{:S(2)}) copy-start(f32[4,32,32]{2,1,0:T(8,128)} %param.27) | copy-start | bytes 49156
  23.9 0.7 copy-start.13
  36.5 1.0 %copy-start.10 = (f32[64,32,128]{2,1,0:T(8,128)}, f32[64,32,128]{2,1,0:T(8,128)S(1)}, u32[]{:S(2)}) copy-start(f32[64,32,128]{2,1,0:T(8,128)S(1)} %fusion.35) | copy-start | bytes 3145732
  43.0 1.0 %copy-start.11 = (f32[64,32,128]{2,1,0:T(8,128)}, f32[64,32,128]{2,1,0:T(8,128)S(1)}, u32[]{:S(2)}) copy-start(f32[64,32,128]{2,1,0:T(8,128)S(1)} %fusion.37) | copy-start | bytes 3145732
  45.4 16.3 %copy-start.2 = (s32[1,128,128]{2,1,0:T(8,128)S(1)}, s32[1,128,128]{2,1,0:T(8,128)}, u32[]{:S(2)}) copy-start(s32[1,128,128]{2,1,0:T(8,128)} %cell_ref.3) | copy-start | bytes 196612
  45.4 16.3 %copy-start.6 = (f32[3,2,4,512]{3,2,1,0:T(4,128)S(1)}, f32[3,2,4,512]{3,2,1,0:T(4,128)}, u32[]{:S(2)}) copy-start(f32[3,2,4,512]{3,2,1,0:T(4,128)} %wind_ref.3) | copy-start | bytes 147460
  45.4 16.3 %all-to-all-start.1 = ((f32[16,8,128]{2,1,0:T(8,128)}), f32[16,8,128]{2,1,0:T(8,128)S(1)}, u32[]{:S(2)}, u32[]{:S(2)}) async-start(f32[16,8,128]{2,1,0:T(8,128)} %bitcast.26), calls=%async_computation.1 | async-start | bytes 131072 | tf_op jit(solution)/shard_map/all_to_all | solution.py:233
  52.3 9.4 %copy-start.7 = (f32[2,4,512]{2,1,0:T(4,128)S(1)}, f32[2,4,512]{2,1,0:T(4,128)}, u32[]{:S(2)}) copy-start(f32[2,4,512]{2,1,0:T(4,128)} %eddy_ref.1) | copy-start | bytes 49156
  52.3 5.2 %collective-permute-start = (f32[2,512]{1,0:T(2,128)S(1)}, f32[2,512]{1,0:T(2,128)S(1)}, u32[]{:S(2)}, u32[]{:S(2)}) collective-permute-start(f32[2,512]{1,0:T(2,128)S(1)} %bitcast.99), channel_id=1, source_target_pairs={{0,2},{2,4},{4,6},{6,8},{8,10},{10,12},{12,14},{14,16},{16,18},{18... | collective-permute-start | bytes 12296 | tf_op jit(solution)/shard_map/ppermute | solution.py:196
  56.1 5.6 %copy-start.9 = (s32[1,128]{1,0:T(1,128)S(1)}, s32[1,128]{1,0:T(1,128)}, u32[]{:S(2)}) copy-start(s32[1,128]{1,0:T(1,128)} %send_ref.3) | copy-start | bytes 1540
  56.2 5.5 %collective-permute-start.1 = (f32[2,512]{1,0:T(2,128)S(1)}, f32[2,512]{1,0:T(2,128)S(1)}, u32[]{:S(2)}, u32[]{:S(2)}) collective-permute-start(f32[2,512]{1,0:T(2,128)S(1)} %bitcast.100), channel_id=1, source_target_pairs={{2,0},{4,2},{6,4},{8,6},{10,8},{12,10},{14,12},{16,14},{18,16},{20... | collective-permute-start | bytes 12296 | tf_op jit(solution)/shard_map/ppermute | solution.py:197

commit v2 on v1

--- a/solution.py
+++ b/solution.py
@@ -1,3 +1,5 @@
+import functools
+
 import jax
 import jax.numpy as jnp
 from jax import lax
@@ -166,6 +168,232 @@
     )(theta, wind, eddy, cells, send, back, *halos)
 
 
+def wall_kernel(
+    count, groups,
+    listed_ref, theta_ref, take_ref, class_ref, wall_ref, inverse_ref, block_ref, pair_ref,
+    wall_out, back_out, low_x_out, high_x_out, low_z_out, high_z_out,
+    recv_ref, flat_ref, edge_ref, edge_got, side_got, district_ref, part_ref, own_part_ref,
+    part_got, matrix_ref, kick_ref, rows_ref, diag_ref, gain_ref, back_ref, back_got,
+    edge_sems, side_sems, emit_sems, part_sems, list_sems, back_sems,
+):
+    me, level = lax.axis_index("xy"), lax.axis_index("gz")
+    levels, x_rows = theta_ref.shape[0], theta_ref.shape[1]
+    capacity = listed_ref.shape[1]
+    owned, nodes, width = wall_ref.shape[1], wall_ref.shape[2], wall_ref.shape[3]
+    classes = inverse_ref.shape[0]
+
+    barrier = pltpu.get_barrier_semaphore()
+    for k in range(1, count):
+        pl.semaphore_signal(
+            barrier, inc=1, device_id={"xy": lax.rem(me + k, count)},
+            device_id_type=pl.DeviceIdType.MESH,
+        )
+    for k in range(1, groups):
+        pl.semaphore_signal(
+            barrier, inc=1, device_id={"gz": lax.rem(level + k, groups)},
+            device_id_type=pl.DeviceIdType.MESH,
+        )
+    pl.semaphore_wait(barrier, count + groups - 2)
+
+    def send(src, dst, sems, at, axis, peer):
+        copy = pltpu.make_async_remote_copy(
+            src_ref=src, dst_ref=dst, send_sem=sems.at[0, at], recv_sem=sems.at[1, at],
+            device_id={axis: peer}, device_id_type=pl.DeviceIdType.MESH,
+        )
+        copy.start()
+        return copy
+
+    list_copies = []
+    for k in range(1, count):
+        peer = lax.rem(me + k, count)
+        list_copies.append(
+            send(listed_ref.at[peer], recv_ref.at[me], list_sems, k - 1, "xy", peer)
+        )
+    first = wall_ref[0, :, 0, :]
+    district_ref[level] = first.astype(jnp.bfloat16)
+    emit_copies = []
+    for k in range(1, groups):
+        peer = lax.rem(level + k, groups)
+        emit_copies.append(
+            send(district_ref.at[level], district_ref.at[level], emit_sems, k - 1, "gz", peer)
+        )
+    edge_ref[0] = theta_ref[:, x_rows - 1, :]
+    edge_ref[1] = theta_ref[:, 0, :]
+    next_x, last_x = lax.rem(me + 1, count), lax.rem(me + count - 1, count)
+    next_z, last_z = lax.rem(level + 1, groups), lax.rem(level + groups - 1, groups)
+    halo_copies = [
+        send(edge_ref.at[0], edge_got.at[0], edge_sems, 0, "xy", next_x),
+        send(edge_ref.at[1], edge_got.at[1], edge_sems, 1, "xy", last_x),
+        send(theta_ref.at[levels - 1], side_got.at[0], side_sems, 0, "gz", next_z),
+        send(theta_ref.at[0], side_got.at[1], side_sems, 1, "gz", last_z),
+    ]
+    recv_ref[me] = listed_ref[me]
+
+    for c in range(classes):
+        a1 = inverse_ref[c]
+        a2 = contract(a1, a1, ((1,), (0,)))
+        a3 = contract(a2, a1, ((1,), (0,)))
+        a4 = contract(a2, a2, ((1,), (0,)))
+        for p, power in enumerate((a1, a2, a3, a4)):
+            kick_ref[c, p] = jnp.broadcast_to(power[:, :1], (nodes, width))
+        stacked = jnp.concatenate((a4, a1[:1], a2[:1], a3[:1], jnp.zeros((5, nodes))), 0)
+        upper = stacked.astype(jnp.bfloat16).astype(jnp.float32)
+        matrix_ref[c] = jnp.concatenate((upper, upper, stacked - upper), 1)
+
+    for copy in emit_copies:
+        copy.wait()
+    total = groups * owned
+    district = district_ref[...].astype(jnp.float32).reshape(total, width)
+    blocks = block_ref.shape[1]
+    row_ids = lax.broadcasted_iota(jnp.int32, (total, blocks), 0)
+    source_hot = (row_ids == pair_ref[0, 1:2, :]).astype(jnp.float32)
+    target_hot = (row_ids == pair_ref[0, 0:1, :]).astype(jnp.float32)
+    source = contract(source_hot, district, ((0,), (0,)))
+    contrib = jnp.concatenate(
+        [
+            lax.dot_general(
+                source[b : b + 1].astype(jnp.bfloat16), block_ref[0, b],
+                (((1,), (1,)), ((), ())), preferred_element_type=jnp.float32,
+            )
+            for b in range(blocks)
+        ],
+        0,
+    )
+    part = contract(target_hot, contrib, ((1,), (0,)))
+    for g in range(groups):
+        own_part_ref[g] = part[g * owned : (g + 1) * owned]
+        part_ref[g] = part[g * owned : (g + 1) * owned].astype(jnp.bfloat16)
+    part_copies = []
+    for k in range(1, groups):
+        peer = lax.rem(level + k, groups)
+        part_copies.append(
+            send(part_ref.at[peer], part_got.at[k - 1], part_sems, k - 1, "gz", peer)
+        )
+
+    def advance(h, carry):
+        t = wall_ref[0, h]
+        kind = class_ref[0, h]
+        upper = t.astype(jnp.bfloat16)
+        lower = (t - upper.astype(jnp.float32)).astype(jnp.bfloat16)
+        got = jnp.dot(
+            matrix_ref[kind].astype(jnp.bfloat16),
+            jnp.concatenate((upper, lower, upper), 0),
+            preferred_element_type=jnp.float32,
+        )
+        wall_out[0, h] = got[:nodes]
+        rows_ref[3, pl.ds(h, 1)] = got[:1]
+        for p in range(3):
+            rows_ref[p, pl.ds(h, 1)] = got[nodes + p : nodes + p + 1]
+        for p in range(SUB):
+            diag_ref[p, pl.ds(h, 1)] = kick_ref[kind, p, :1, :]
+        return carry
+
+    lax.fori_loop(0, owned, advance, 0, unroll=4)
+
+    for copy in part_copies:
+        copy.wait()
+    rad = own_part_ref[level]
+    for k in range(groups - 1):
+        rad = rad + part_got[k].astype(jnp.float32)
+    for copy in list_copies:
+        copy.wait()
+    for j in range(count):
+        flat_ref[j * capacity : (j + 1) * capacity, :] = recv_ref[j]
+    take_hot = (
+        lax.broadcasted_iota(jnp.int32, (count * capacity, owned), 0) == take_ref[...]
+    ).astype(jnp.float32)
+    both = contract(take_hot, flat_ref[...], ((0,), (0,)))
+    air, coef = both[:, :width], both[:, width:]
+    surface, gains = first, []
+    for step in range(SUB):
+        gains.append(wall_gain * (coef * (air - surface) + rad))
+        gain_ref[step] = gains[step]
+        surface = rows_ref[step]
+        for q in range(step + 1):
+            surface = surface + diag_ref[step - q] * gains[q]
+    back = contract(take_hot, coef * (surface - air), ((1,), (0,)))
+    for j in range(count):
+        back_ref[j] = back[j * capacity : (j + 1) * capacity]
+    back_copies = []
+    for k in range(1, count):
+        peer = lax.rem(me + k, count)
+        back_copies.append(
+            send(back_ref.at[peer], back_got.at[me], back_sems, k - 1, "xy", peer)
+        )
+    back_got[me] = back_ref[me]
+
+    def finish(h, carry):
+        kind = class_ref[0, h]
+        t = wall_out[0, h]
+        for q in range(SUB):
+            t = t + kick_ref[kind, SUB - 1 - q] * gain_ref[q, pl.ds(h, 1)]
+        wall_out[0, h] = t
+        return carry
+
+    lax.fori_loop(0, owned, finish, 0, unroll=4)
+
+    for copy in halo_copies:
+        copy.wait()
+    low_x_out[...] = edge_got[0] * (me > 0).astype(jnp.float32)
+    high_x_out[...] = edge_got[1] * (me < count - 1).astype(jnp.float32)
+    low_z_out[...] = side_got[0] * (level > 0).astype(jnp.float32)
+    high_z_out[...] = side_got[1] * (level < groups - 1).astype(jnp.float32)
+    for copy in back_copies:
+        copy.wait()
+    back_out[...] = back_got[...]
+
+
+def call_wall(listed, theta, take, kinds, wall, inverse, blocks, pairs):
+    count, groups = lax.axis_size("xy"), lax.axis_size("gz")
+    capacity = listed.shape[1]
+    owned, nodes, width = wall.shape[1:]
+    levels, x_rows, y_cells = theta.shape
+    classes = inverse.shape[0]
+    f32, bf16 = jnp.float32, jnp.bfloat16
+    vmem = pl.BlockSpec(memory_space=pltpu.VMEM)
+    smem = pl.BlockSpec(memory_space=pltpu.SMEM)
+    x_side = jax.ShapeDtypeStruct((levels, y_cells), f32)
+    z_side = jax.ShapeDtypeStruct((x_rows, y_cells), f32)
+
+    def pairs_of(n):
+        return pltpu.SemaphoreType.DMA((2, n))
+
+    return pl.pallas_call(
+        functools.partial(wall_kernel, count, groups),
+        out_shape=(
+            jax.ShapeDtypeStruct(wall.shape, f32),
+            jax.ShapeDtypeStruct((count, capacity, width), f32),
+            x_side, x_side, z_side, z_side,
+        ),
+        in_specs=[vmem, vmem, vmem, smem, vmem, vmem, vmem, vmem],
+        out_specs=(vmem,) * 6,
+        scratch_shapes=[
+            pltpu.VMEM(listed.shape, f32),
+            pltpu.VMEM((count * capacity, 2 * width), f32),
+            pltpu.VMEM((2, levels, y_cells), f32),
+            pltpu.VMEM((2, levels, y_cells), f32),
+            pltpu.VMEM((2, x_rows, y_cells), f32),
+            pltpu.VMEM((groups, owned, width), bf16),
+            pltpu.VMEM((groups, owned, width), bf16),
+            pltpu.VMEM((groups, owned, width), f32),
+            pltpu.VMEM((groups - 1, owned, width), bf16),
+            pltpu.VMEM((classes, nodes + 8, 3 * nodes), f32),
+            pltpu.VMEM((classes, SUB, nodes, width), f32),
+            pltpu.VMEM((SUB, owned, width), f32),
+            pltpu.VMEM((SUB, owned, width), f32),
+            pltpu.VMEM((SUB, owned, width), f32),
+            pltpu.VMEM((count, capacity, width), f32),
+            pltpu.VMEM((count, capacity, width), f32),
+            pairs_of(2), pairs_of(2), pairs_of(groups - 1), pairs_of(groups - 1),
+            pairs_of(count - 1), pairs_of(count - 1),
+        ],
+        compiler_params=pltpu.CompilerParams(
+            collective_id=0, has_side_effects=True, vmem_limit_bytes=VMEM_LIMIT
+        ),
+        name="wall",
+    )(listed, theta, take, kinds, wall, inverse, blocks, pairs)
+
+
 def on_device(
     potential_temp,
     wind_field,
@@ -179,64 +407,16 @@
     refl_block,
     refl_pair,
 ):
-    levels, x_rows, y_cells = potential_temp.shape
-    tile_slots = facade_cell.shape[1]
-    tile_width = facade_cell.shape[2]
-    owned = tile_take.shape[1]
-    node_count = wall_temp.shape[2]
     xy_count = lax.axis_size("xy")
-    capacity = 2 * owned // xy_count
-    slot_total = xy_count * capacity
+    capacity = 2 * tile_take.shape[1] // xy_count
     listed = call_lookup(potential_temp, wind_field, facade_cell, tile_send, xy_count, capacity)
-    halos = []
-    for axis, dim in (("xy", 1), ("gz", 0)):
-        size, length = lax.axis_size(axis), potential_temp.shape[dim]
-        up = [(i, i + 1) for i in range(size - 1)]
-        down = [(j, i) for i, j in up]
-        halos.append(lax.ppermute(lax.index_in_dim(potential_temp, length - 1, dim, False), axis, up))
-        halos.append(lax.ppermute(lax.index_in_dim(potential_temp, 0, dim, False), axis, down))
-    received = lax.all_to_all(listed, "xy", split_axis=0, concat_axis=0, tiled=True)
-    received = received.reshape(slot_total, 2 * tile_width)
-    take_rows = tile_take.reshape(owned)
-    own_both = received[take_rows]
-    own_air, own_coef = own_both[:, :tile_width], own_both[:, tile_width:]
-    wall_state = wall_temp.reshape(owned, node_count, tile_width)
-    emitted = wall_state[:, 0, :].astype(jnp.bfloat16)
-    district = lax.all_gather(emitted, "gz", axis=0, tiled=True)
-    blocks = refl_block[0]
-    pair_rows = refl_pair[0]
-    source_emit = district[pair_rows[1]]
-    contrib = jnp.einsum("bij,bj->bi", blocks, source_emit, preferred_element_type=jnp.float32)
-    targets = pair_rows[0]
-    district_rows = lax.axis_size("gz") * owned
-    row_ids = lax.iota(jnp.int32, district_rows)
-    one_hot = (row_ids[:, None] == targets[None, :]).astype(jnp.float32)
-    whole = lax.psum(
-        jnp.dot(
-            one_hot, contrib, precision=lax.Precision.HIGHEST, preferred_element_type=jnp.float32
-        ).astype(jnp.bfloat16),
-        "gz",
-    ).astype(jnp.float32)
-    own_rad = lax.dynamic_slice_in_dim(whole, lax.axis_index("gz") * owned, owned, 0)
-    class_ids = lax.broadcasted_iota(jnp.int32, (owned, wall_inverse.shape[0]), 1)
-    class_hot = (wall_class.reshape(owned)[:, None] == class_ids).astype(jnp.float32)
-    inverse_tile = jnp.einsum(
-        "tc,cab->tab", class_hot, wall_inverse, precision=lax.Precision.HIGHEST
-    )
-    temps = wall_state
-    for substep in range(SUB):
-        forcing = own_coef * (own_air - temps[:, 0, :]) + own_rad
-        temps = temps.at[:, 0, :].add(wall_gain * forcing)
-        temps = jnp.einsum("tab,tbf->taf", inverse_tile, temps, precision=lax.Precision.HIGHEST)
-    flux_out = own_coef * (temps[:, 0, :] - own_air)
-    back_rows = jnp.zeros((slot_total, tile_width), jnp.float32).at[take_rows].set(flux_out)
-    returned = lax.all_to_all(
-        back_rows.reshape(xy_count, capacity, tile_width), "xy", split_axis=0, concat_axis=0, tiled=True
+    wall_next, returned, *halos = call_wall(
+        listed, potential_temp, tile_take, wall_class, wall_temp, wall_inverse, refl_block, refl_pair
     )
     temp_next = call_heat(
         potential_temp, wind_field, eddy_diff, facade_cell, tile_send, returned, halos
     )
-    return (temp_next, temps.reshape(1, owned, node_count, tile_width))
+    return (temp_next, wall_next)
 
 
 def solution(mesh):

time: 67.3 us -> 33.3 us (0.49)
  starting transfers between devices: 23.2 us -> 0 us
  Pallas kernels: 7.75 us -> 25.9 us
  matrix products: 8.78 us -> 0 us
  local copies, waits for them, and re-layouts: 12.9 us -> 6.25 us
  blocking collectives: 6.32 us -> 0 us
  waiting for transfers between devices: 4.2 us -> 0 us
  other arithmetic: 2.03 us -> 0 us
    pallas_call x0 -> x1, Pallas kernels: none -> 18.8 us  [call_wall(): pl.pallas_call(functools.partial(wall_kernel, count, groups), out_shape=(...]
    all_to_all x2 -> x0, starting transfers between devices: 15.3 us -> none  [the longest x1 8.44 us: on_device(): lax.all_to_all(listed, 'xy', split_axis=0, concat_axis=0, tiled=True)]
    dot_general x7 -> x0, matrix products: 8.78 us -> none  [the longest x4 7.61 us: on_device(): jnp.einsum('tab,tbf->taf', inverse_tile, temps, precision=lax.Precision.H...]
    ppermute x4 -> x0, starting transfers between devices: 7.87 us -> none  [the longest x2 5.28 us: on_device(): lax.ppermute(lax.index_in_dim(potential_temp, length - 1, dim, False), ax...]
    ppermute x4 -> x0, waiting for transfers between devices: 4.2 us -> none  [the longest x2 4.19 us: on_device(): lax.ppermute(lax.index_in_dim(potential_temp, 0, dim, False), axis, down)]
    psum x1 -> x0, blocking collectives: 3.58 us -> none  [on_device(): lax.psum(jnp.dot(one_hot, contrib, precision=lax.Precision.HIGHEST, prefe...]
    all_gather x1 -> x0, blocking collectives: 2.73 us -> none  [on_device(): district = lax.all_gather(emitted, 'gz', axis=0, tiled=True)]
    unnamed x36 -> x23, local copies, waits for them, and re-layouts: 8.5 us -> 6.25 us
  transfers between devices with their start and end apart: 6 -> 0, of which waited for: 1 -> 0; matrix products, arithmetic and copies ran while one was open for 27% -> 0% of each run, Pallas kernels for 0% -> 0%
where the time goes in v2:
time: 33.3 us; the launch traced here: 32.9 us
  Pallas kernels  25.9 us (78%)
  local copies, waits for them, and re-layouts  6.25 us (19%)
  between operations  0.71 us (2%)
    pallas_call x1, Pallas kernels, call_wall(): pl.pallas_call(functools.partial(wall_kernel, count, groups), out_shape=(...  18.8 us
    unnamed x23, local copies, waits for them, and re-layouts  6.25 us
    pallas_call x1, Pallas kernels, call_heat(): pl.pallas_call(heat_kernel, out_shape=jax.ShapeDtypeStruct(theta.shape, j...  4.51 us
    pallas_call x1, Pallas kernels, call_lookup(): pl.pallas_call(lookup_kernel, out_shape=jax.ShapeDtypeStruct((count, capa...  2.6 us

profile of v2, /device:TPU:0, one launch (start us, length us, event | category | flops | bytes accessed | tf_op | source)
XLA Modules:
  0.0 32.9 jit_solution(11435168510330806173)
XLA Ops:
  0.6 0.0 copy-start.2
  0.6 0.8 %copy-done.2 = s32[1,128,128]{2,1,0:T(8,128)S(1)} copy-done((s32[1,128,128]{2,1,0:T(8,128)S(1)}, s32[1,128,128]{2,1,0:T(8,128)}, u32[]{:S(2)}) %copy-start.2) | copy-done | bytes 65560
  1.5 0.0 copy-start.3
  1.5 0.8 %copy-done.3 = f32[3,2,4,512]{3,2,1,0:T(4,128)S(1)} copy-done((f32[3,2,4,512]{3,2,1,0:T(4,128)S(1)}, f32[3,2,4,512]{3,2,1,0:T(4,128)}, u32[]{:S(2)}) %copy-start.3) | copy-done | bytes 49176
  2.3 0.0 copy-start.4
  2.3 0.7 %copy-done.4 = f32[2,4,512]{2,1,0:T(4,128)S(1)} copy-done((f32[2,4,512]{2,1,0:T(4,128)S(1)}, f32[2,4,512]{2,1,0:T(4,128)}, u32[]{:S(2)}) %copy-start.4) | copy-done | bytes 16408
  3.0 0.0 copy-start.7
  3.0 0.7 %copy-done.7 = s32[1,128]{1,0:T(1,128)S(1)} copy-done((s32[1,128]{1,0:T(1,128)S(1)}, s32[1,128]{1,0:T(1,128)}, u32[]{:S(2)}) %copy-start.7) | copy-done | bytes 536
  3.6 0.0 copy-start.5
  3.6 0.0 copy-start.8
  3.6 0.0 copy-start.9
  3.7 0.0 copy-start.10
  3.7 2.6 %lookup.1.listed_ref = f32[16,8,256]{2,1,0:T(8,128)S(1)} custom-call(f32[2,4,512]{2,1,0:T(4,128)S(1)} %copy-done.4, f32[3,2,4,512]{3,2,1,0:T(4,128)S(1)} %copy-done.3, s32[1,128,128]{2,1,0:T(8,128)S(1)} %copy-done.2, s32[1,128]{1,0:T(1,128)S(1)} %copy-done.7), custom_call_target="tpu_custom_call" | custom-call | tf_op jit(solution)/shard_map/lookup/pallas_call | solution.py:141
  6.3 0.0 copy-done.5
  6.3 0.0 copy-done.8
  6.3 0.0 copy-done.9
  6.3 0.0 copy-done.10
  6.3 0.0 copy-start
  6.3 1.2 %copy-done = f32[1,64,32,128]{3,2,1,0:T(8,128)S(1)} copy-done((f32[1,64,32,128]{3,2,1,0:T(8,128)S(1)}, f32[1,64,32,128]{3,2,1,0:T(8,128)}, u32[]{:S(2)}) %copy-start) | copy-done | bytes 1048600
  7.5 0.0 copy-start.1
  7.5 1.0 %copy-done.1 = bf16[1,16,128,128]{3,2,1,0:T(8,128)(2,1)S(1)} copy-done((bf16[1,16,128,128]{3,2,1,0:T(8,128)(2,1)S(1)}, bf16[1,16,128,128]{3,2,1,0:T(8,128)(2,1)}, u32[]{:S(2)}) %copy-start.1) | copy-done | bytes 524312
  8.6 0.0 copy-start.6
  8.6 18.8 %wall.1 = (f32[1,64,32,128]{3,2,1,0:T(8,128)S(1)}, f32[16,8,128]{2,1,0:T(8,128)S(1)}, f32[2,512]{1,0:T(2,128)S(1)}, f32[2,512]{1,0:T(2,128)S(1)}, f32[4,512]{1,0:T(4,128)S(1)}, /*index=5*/f32[4,512]{1,0:T(4,128)S(1)}) custom-call(f32[16,8,256]{2,1,0:T(8,128)S(1)} %lookup.1.listed_ref, f32[2,4,512]{2,1,0:T(4,128)S(1)} %copy-done.4, s32[1,64]{1,0:T(1,128)S(1)} %copy-done.9, ...), custom_call_target="tpu_custom_call" | custom-call | tf_op jit(solution)/shard_map/wall/pallas_call | solution.py:361
  27.4 0.0 copy-done.6
  27.4 4.5 %heat.1 = f32[2,4,512]{2,1,0:T(4,128)} custom-call(f32[2,4,512]{2,1,0:T(4,128)S(1)} %copy-done.4, f32[3,2,4,512]{3,2,1,0:T(4,128)S(1)} %copy-done.3, f32[2,4,512]{2,1,0:T(4,128)S(1)} %copy-done.6, s32[1,128,128]{2,1,0:T(8,128)S(1)} %copy-done.2, s32[1,128]{1,0:T(1,128)S(1)} %copy-done.7, f32[16,8,128]{2,1,0:T(8,128)S(1)} %get-tuple-element.8.back_ref, ...), custom_call_target="tpu_custom_call" | custom-call | tf_op jit(solution)/shard_map/heat/pallas_call | solution.py:157
  31.9 1.0 %copy.14 = f32[1,64,32,128]{3,2,1,0:T(8,128)} copy(f32[1,64,32,128]{3,2,1,0:T(8,128)S(1)} %get-tuple-element.17) | data formatting | bytes 2097152
Async XLA Ops:
  0.6 0.8 %copy-start.2 = (s32[1,128,128]{2,1,0:T(8,128)S(1)}, s32[1,128,128]{2,1,0:T(8,128)}, u32[]{:S(2)}) copy-start(s32[1,128,128]{2,1,0:T(8,128)} %cell_ref.3) | copy-start | bytes 196612
  1.5 0.8 %copy-start.3 = (f32[3,2,4,512]{3,2,1,0:T(4,128)S(1)}, f32[3,2,4,512]{3,2,1,0:T(4,128)}, u32[]{:S(2)}) copy-start(f32[3,2,4,512]{3,2,1,0:T(4,128)} %wind_ref.3) | copy-start | bytes 147460
  2.3 0.7 %copy-start.4 = (f32[2,4,512]{2,1,0:T(4,128)S(1)}, f32[2,4,512]{2,1,0:T(4,128)}, u32[]{:S(2)}) copy-start(f32[2,4,512]{2,1,0:T(4,128)} %theta_ref.5) | copy-start | bytes 49156
  3.0 0.7 %copy-start.7 = (s32[1,128]{1,0:T(1,128)S(1)}, s32[1,128]{1,0:T(1,128)}, u32[]{:S(2)}) copy-start(s32[1,128]{1,0:T(1,128)} %send_ref.3) | copy-start | bytes 1540
  3.6 2.6 %copy-start.5 = (f32[4,32,32]{2,1,0:T(8,128)S(1)}, f32[4,32,32]{2,1,0:T(8,128)}, u32[]{:S(2)}) copy-start(f32[4,32,32]{2,1,0:T(8,128)} %inverse_ref.1) | copy-start | bytes 49156
  3.6 2.6 %copy-start.8 = (s32[1,2,16]{2,1,0:T(2,128)S(1)}, s32[1,2,16]{2,1,0:T(2,128)}, u32[]{:S(2)}) copy-start(s32[1,2,16]{2,1,0:T(2,128)} %pair_ref.1) | copy-start | bytes 388
  3.6 2.6 %copy-start.9 = (s32[1,64]{1,0:T(1,128)S(1)}, s32[1,64]{1,0:T(1,128)}, u32[]{:S(2)}) copy-start(s32[1,64]{1,0:T(1,128)} %take_ref.1) | copy-start | bytes 772
  3.7 2.6 %copy-start.10 = (s32[1,64]{1,0:T(1,128)S(1)}, s32[1,64]{1,0:T(1,128)}, u32[]{:S(2)}) copy-start(s32[1,64]{1,0:T(1,128)} %class_ref.1) | copy-start | bytes 772
  6.3 1.2 %copy-start = (f32[1,64,32,128]{3,2,1,0:T(8,128)S(1)}, f32[1,64,32,128]{3,2,1,0:T(8,128)}, u32[]{:S(2)}) copy-start(f32[1,64,32,128]{3,2,1,0:T(8,128)} %wall_ref.1) | copy-start | bytes 3145732
  7.5 1.0 %copy-start.1 = (bf16[1,16,128,128]{3,2,1,0:T(8,128)(2,1)S(1)}, bf16[1,16,128,128]{3,2,1,0:T(8,128)(2,1)}, u32[]{:S(2)}) copy-start(bf16[1,16,128,128]{3,2,1,0:T(8,128)(2,1)} %block_ref.1) | copy-start | bytes 1572868
  8.6 18.8 %copy-start.6 = (f32[2,4,512]{2,1,0:T(4,128)S(1)}, f32[2,4,512]{2,1,0:T(4,128)}, u32[]{:S(2)}) copy-start(f32[2,4,512]{2,1,0:T(4,128)} %eddy_ref.1) | copy-start | bytes 49156

commit v3 on v2

--- a/solution.py
+++ b/solution.py
@@ -20,7 +20,7 @@
 
 LANES = 128
 HIGH = lax.Precision.HIGHEST
-VMEM_LIMIT = 40 * 1024 * 1024
+LOOKUP_VMEM, HEAT_VMEM, WALL_VMEM = (n * 1024 * 1024 for n in (60, 60, 60))
 
 
 def contract(a, b, dims):
@@ -35,7 +35,28 @@
     return (row_ids == send_ref[...]).astype(jnp.float32)
 
 
-def lookup_kernel(theta_ref, wind_ref, cell_ref, send_ref, out_ref, coef_ref, found_ref):
+def fetch(pairs, sems):
+    copies = [
+        pltpu.make_async_copy(src, dst, sems.at[n]) for n, (src, dst) in enumerate(pairs)
+    ]
+    for copy in copies:
+        copy.start()
+    return copies
+
+
+def lookup_kernel(
+    theta_hbm, wind_hbm, cell_hbm, send_hbm, out_ref,
+    theta_ref, wind_ref, cell_ref, send_ref, coef_ref, found_ref, sems,
+):
+    copies = fetch(
+        (
+            (theta_hbm, theta_ref), (wind_hbm, wind_ref), (cell_hbm, cell_ref),
+            (send_hbm, send_ref),
+        ),
+        sems,
+    )
+    for copy in copies:
+        copy.wait()
     levels, rows, y_cells = theta_ref.shape
     slots, width = found_ref.shape[0], found_ref.shape[1] // 2
     pieces = y_cells // LANES
@@ -71,8 +92,11 @@
 
 def heat_kernel(
     theta_ref, wind_ref, eddy_ref, cell_ref, send_ref, back_ref,
-    low_x_ref, high_x_ref, low_z_ref, high_z_ref, out_ref, rows_ref, flux_ref,
+    low_x_ref, high_x_ref, low_z_ref, high_z_ref, wall_ref, out_ref, wall_out,
+    rows_ref, flux_ref, sem,
 ):
+    wall_copy = pltpu.make_async_copy(wall_ref, wall_out, sem)
+    wall_copy.start()
     levels, rows, y_cells = theta_ref.shape
     lines, pieces = levels * rows, y_cells // LANES
     slots, width = flux_ref.shape
@@ -134,6 +158,7 @@
         out_ref[z] = (
             c - advect + eddy_ref[z] * laplace + flux_gain * heat[z * rows : (z + 1) * rows]
         )
+    wall_copy.wait()
 
 
 def call_lookup(theta, wind, cells, send, count, capacity):
@@ -141,40 +166,53 @@
     return pl.pallas_call(
         lookup_kernel,
         out_shape=jax.ShapeDtypeStruct((count, capacity, 2 * width), jnp.float32),
-        in_specs=[pl.BlockSpec(memory_space=pltpu.VMEM)] * 4,
+        in_specs=[pl.BlockSpec(memory_space=pltpu.HBM)] * 4,
         out_specs=pl.BlockSpec(memory_space=pltpu.VMEM),
         scratch_shapes=[
             pltpu.VMEM(theta.shape, jnp.float32),
+            pltpu.VMEM(wind.shape, jnp.float32),
+            pltpu.VMEM(cells.shape, jnp.int32),
+            pltpu.VMEM(send.shape, jnp.int32),
+            pltpu.VMEM(theta.shape, jnp.float32),
             pltpu.VMEM((slots, 2 * width), jnp.float32),
+            pltpu.SemaphoreType.DMA((4,)),
         ],
-        compiler_params=pltpu.CompilerParams(vmem_limit_bytes=VMEM_LIMIT),
+        compiler_params=pltpu.CompilerParams(vmem_limit_bytes=LOOKUP_VMEM),
         name="lookup",
     )(theta, wind, cells, send)
 
 
-def call_heat(theta, wind, eddy, cells, send, back, halos):
+def call_heat(theta, wind, eddy, cells, send, back, halos, wall):
     slots, width = cells.shape[1], cells.shape[2]
     return pl.pallas_call(
         heat_kernel,
-        out_shape=jax.ShapeDtypeStruct(theta.shape, jnp.float32),
-        in_specs=[pl.BlockSpec(memory_space=pltpu.VMEM)] * 10,
-        out_specs=pl.BlockSpec(memory_space=pltpu.VMEM),
+        out_shape=(
+            jax.ShapeDtypeStruct(theta.shape, jnp.float32),
+            jax.ShapeDtypeStruct(wall.shape, jnp.float32),
+        ),
+        in_specs=[pl.BlockSpec(memory_space=pltpu.VMEM)] * 10
+        + [pl.BlockSpec(memory_space=pl.ANY)],
+        out_specs=(
+            pl.BlockSpec(memory_space=pltpu.VMEM), pl.BlockSpec(memory_space=pltpu.HBM),
+        ),
         scratch_shapes=[
             pltpu.VMEM((back.shape[0] * back.shape[1], width), jnp.float32),
             pltpu.VMEM((slots, width), jnp.float32),
+            pltpu.SemaphoreType.DMA(()),
         ],
-        compiler_params=pltpu.CompilerParams(vmem_limit_bytes=VMEM_LIMIT),
+        compiler_params=pltpu.CompilerParams(vmem_limit_bytes=HEAT_VMEM),
         name="heat",
-    )(theta, wind, eddy, cells, send, back, *halos)
+    )(theta, wind, eddy, cells, send, back, *halos, wall)
 
 
 def wall_kernel(
     count, groups,
-    listed_ref, theta_ref, take_ref, class_ref, wall_ref, inverse_ref, block_ref, pair_ref,
+    listed_ref, theta_hbm, take_hbm, class_ref, wall_hbm, inverse_hbm, block_hbm, pair_hbm,
     wall_out, back_out, low_x_out, high_x_out, low_z_out, high_z_out,
     recv_ref, flat_ref, edge_ref, edge_got, side_got, district_ref, part_ref, own_part_ref,
     part_got, matrix_ref, kick_ref, rows_ref, diag_ref, gain_ref, back_ref, back_got,
     edge_sems, side_sems, emit_sems, part_sems, list_sems, back_sems,
+    theta_ref, take_ref, wall_ref, inverse_ref, block_ref, pair_ref, fetch_sems,
 ):
     me, level = lax.axis_index("xy"), lax.axis_index("gz")
     levels, x_rows = theta_ref.shape[0], theta_ref.shape[1]
@@ -182,6 +220,13 @@
     owned, nodes, width = wall_ref.shape[1], wall_ref.shape[2], wall_ref.shape[3]
     classes = inverse_ref.shape[0]
 
+    fetches = fetch(
+        (
+            (theta_hbm, theta_ref), (wall_hbm, wall_ref), (inverse_hbm, inverse_ref),
+            (take_hbm, take_ref), (pair_hbm, pair_ref), (block_hbm, block_ref),
+        ),
+        fetch_sems,
+    )
     barrier = pltpu.get_barrier_semaphore()
     for k in range(1, count):
         pl.semaphore_signal(
@@ -209,6 +254,8 @@
         list_copies.append(
             send(listed_ref.at[peer], recv_ref.at[me], list_sems, k - 1, "xy", peer)
         )
+    for copy in fetches:
+        copy.wait()
     first = wall_ref[0, :, 0, :]
     district_ref[level] = first.astype(jnp.bfloat16)
     emit_copies = []
@@ -351,6 +398,7 @@
     classes = inverse.shape[0]
     f32, bf16 = jnp.float32, jnp.bfloat16
     vmem = pl.BlockSpec(memory_space=pltpu.VMEM)
+    hbm = pl.BlockSpec(memory_space=pltpu.HBM)
     smem = pl.BlockSpec(memory_space=pltpu.SMEM)
     x_side = jax.ShapeDtypeStruct((levels, y_cells), f32)
     z_side = jax.ShapeDtypeStruct((x_rows, y_cells), f32)
@@ -365,7 +413,7 @@
             jax.ShapeDtypeStruct((count, capacity, width), f32),
             x_side, x_side, z_side, z_side,
         ),
-        in_specs=[vmem, vmem, vmem, smem, vmem, vmem, vmem, vmem],
+        in_specs=[vmem, hbm, hbm, smem, hbm, hbm, hbm, hbm],
         out_specs=(vmem,) * 6,
         scratch_shapes=[
             pltpu.VMEM(listed.shape, f32),
@@ -386,9 +434,11 @@
             pltpu.VMEM((count, capacity, width), f32),
             pairs_of(2), pairs_of(2), pairs_of(groups - 1), pairs_of(groups - 1),
             pairs_of(count - 1), pairs_of(count - 1),
+            *(pltpu.VMEM(a.shape, a.dtype) for a in (theta, take, wall, inverse, blocks, pairs)),
+            pltpu.SemaphoreType.DMA((6,)),
         ],
         compiler_params=pltpu.CompilerParams(
-            collective_id=0, has_side_effects=True, vmem_limit_bytes=VMEM_LIMIT
+            collective_id=0, has_side_effects=True, vmem_limit_bytes=WALL_VMEM
         ),
         name="wall",
     )(listed, theta, take, kinds, wall, inverse, blocks, pairs)
@@ -410,13 +460,12 @@
     xy_count = lax.axis_size("xy")
     capacity = 2 * tile_take.shape[1] // xy_count
     listed = call_lookup(potential_temp, wind_field, facade_cell, tile_send, xy_count, capacity)
-    wall_next, returned, *halos = call_wall(
+    wall_done, returned, *halos = call_wall(
         listed, potential_temp, tile_take, wall_class, wall_temp, wall_inverse, refl_block, refl_pair
     )
-    temp_next = call_heat(
-        potential_temp, wind_field, eddy_diff, facade_cell, tile_send, returned, halos
-    )
-    return (temp_next, wall_next)
+    return call_heat(
+        potential_temp, wind_field, eddy_diff, facade_cell, tile_send, returned, halos, wall_done
+    )
 
 
 def solution(mesh):

time: 33.3 us -> 59.7 us (1.79)
  Pallas kernels: 25.9 us -> 58.8 us
  local copies, waits for them, and re-layouts: 6.25 us -> 0 us
    pallas_call x1, Pallas kernels: 4.51 us -> 34.4 us  [call_heat(): pl.pallas_call(heat_kernel, out_shape=(jax.ShapeDtypeStruct(theta.shape,...]
    unnamed x23 -> x0, local copies, waits for them, and re-layouts: 6.25 us -> none
    pallas_call x1, Pallas kernels: 2.6 us -> 4.18 us  [call_lookup(): pl.pallas_call(lookup_kernel, out_shape=jax.ShapeDtypeStruct((count, capa...]
    pallas_call x1, Pallas kernels: 18.8 us -> 20.3 us  [call_wall(): pl.pallas_call(functools.partial(wall_kernel, count, groups), out_shape=(...]
where the time goes in v3:
time: 59.7 us; the launch traced here: 59.5 us
  Pallas kernels  58.8 us (98%)
  between operations  0.64 us (1%)
    pallas_call x1, Pallas kernels, call_heat(): pl.pallas_call(heat_kernel, out_shape=(jax.ShapeDtypeStruct(theta.shape,...  34.4 us
    pallas_call x1, Pallas kernels, call_wall(): pl.pallas_call(functools.partial(wall_kernel, count, groups), out_shape=(...  20.3 us
    pallas_call x1, Pallas kernels, call_lookup(): pl.pallas_call(lookup_kernel, out_shape=jax.ShapeDtypeStruct((count, capa...  4.18 us

profile of v3, /device:TPU:0, one launch (start us, length us, event | category | flops | bytes accessed | tf_op | source)
XLA Modules:
  0.0 59.5 jit_solution(875284199325933313)
XLA Ops:
  0.6 4.2 %lookup.1.listed_ref = f32[16,8,256]{2,1,0:T(8,128)} custom-call(f32[2,4,512]{2,1,0:T(4,128)} %theta_ref.1, f32[3,2,4,512]{3,2,1,0:T(4,128)} %wind_ref.1, s32[1,128,128]{2,1,0:T(8,128)} %cell_ref.1, s32[1,128]{1,0:T(1,128)} %send_ref.1), custom_call_target="tpu_custom_call" | custom-call | tf_op jit(solution)/shard_map/lookup/pallas_call | solution.py:166
  4.8 20.3 %wall.1 = (f32[1,64,32,128]{3,2,1,0:T(8,128)}, f32[16,8,128]{2,1,0:T(8,128)}, f32[2,512]{1,0:T(2,128)}, f32[2,512]{1,0:T(2,128)}, f32[4,512]{1,0:T(4,128)}, /*index=5*/f32[4,512]{1,0:T(4,128)}) custom-call(f32[16,8,256]{2,1,0:T(8,128)} %lookup.1.listed_ref, f32[2,4,512]{2,1,0:T(4,128)} %theta_ref.1, s32[1,64]{1,0:T(1,128)} %take_hbm.1, s32[1,64]{1,0:T(1,128)} %class_ref.1, ...), custom_call_target="tpu_custom_call" | custom-call | tf_op jit(solution)/shard_map/wall/pallas_call | solution.py:409
  25.1 34.4 %heat.1 = (f32[2,4,512]{2,1,0:T(4,128)}, f32[1,64,32,128]{3,2,1,0:T(8,128)}) custom-call(f32[2,4,512]{2,1,0:T(4,128)} %theta_ref.1, f32[3,2,4,512]{3,2,1,0:T(4,128)} %wind_ref.1, f32[2,4,512]{2,1,0:T(4,128)} %eddy_ref.1, s32[1,128,128]{2,1,0:T(8,128)} %cell_ref.1, s32[1,128]{1,0:T(1,128)} %send_ref.1, f32[16,8,128]{2,1,0:T(8,128)} %get-tuple-element.8.back_ref, ...), custom_call_target="tpu_custom_call" | custom-call | tf_op jit(solution)/shard_map/heat/pallas_call | solution.py:187

commit v4 on v3

--- a/solution.py
+++ b/solution.py
@@ -92,11 +92,9 @@
 
 def heat_kernel(
     theta_ref, wind_ref, eddy_ref, cell_ref, send_ref, back_ref,
-    low_x_ref, high_x_ref, low_z_ref, high_z_ref, wall_ref, out_ref, wall_out,
-    rows_ref, flux_ref, sem,
+    low_x_ref, high_x_ref, low_z_ref, high_z_ref, out_ref,
+    rows_ref, flux_ref,
 ):
-    wall_copy = pltpu.make_async_copy(wall_ref, wall_out, sem)
-    wall_copy.start()
     levels, rows, y_cells = theta_ref.shape
     lines, pieces = levels * rows, y_cells // LANES
     slots, width = flux_ref.shape
@@ -158,7 +156,6 @@
         out_ref[z] = (
             c - advect + eddy_ref[z] * laplace + flux_gain * heat[z * rows : (z + 1) * rows]
         )
-    wall_copy.wait()
 
 
 def call_lookup(theta, wind, cells, send, count, capacity):
@@ -182,27 +179,20 @@
     )(theta, wind, cells, send)
 
 
-def call_heat(theta, wind, eddy, cells, send, back, halos, wall):
+def call_heat(theta, wind, eddy, cells, send, back, halos):
     slots, width = cells.shape[1], cells.shape[2]
     return pl.pallas_call(
         heat_kernel,
-        out_shape=(
-            jax.ShapeDtypeStruct(theta.shape, jnp.float32),
-            jax.ShapeDtypeStruct(wall.shape, jnp.float32),
-        ),
-        in_specs=[pl.BlockSpec(memory_space=pltpu.VMEM)] * 10
-        + [pl.BlockSpec(memory_space=pl.ANY)],
-        out_specs=(
-            pl.BlockSpec(memory_space=pltpu.VMEM), pl.BlockSpec(memory_space=pltpu.HBM),
-        ),
+        out_shape=jax.ShapeDtypeStruct(theta.shape, jnp.float32),
+        in_specs=[pl.BlockSpec(memory_space=pltpu.VMEM)] * 10,
+        out_specs=pl.BlockSpec(memory_space=pltpu.VMEM),
         scratch_shapes=[
             pltpu.VMEM((back.shape[0] * back.shape[1], width), jnp.float32),
             pltpu.VMEM((slots, width), jnp.float32),
-            pltpu.SemaphoreType.DMA(()),
         ],
         compiler_params=pltpu.CompilerParams(vmem_limit_bytes=HEAT_VMEM),
         name="heat",
-    )(theta, wind, eddy, cells, send, back, *halos, wall)
+    )(theta, wind, eddy, cells, send, back, *halos)
 
 
 def wall_kernel(
@@ -460,12 +450,13 @@
     xy_count = lax.axis_size("xy")
     capacity = 2 * tile_take.shape[1] // xy_count
     listed = call_lookup(potential_temp, wind_field, facade_cell, tile_send, xy_count, capacity)
-    wall_done, returned, *halos = call_wall(
+    wall_next, returned, *halos = call_wall(
         listed, potential_temp, tile_take, wall_class, wall_temp, wall_inverse, refl_block, refl_pair
     )
-    return call_heat(
-        potential_temp, wind_field, eddy_diff, facade_cell, tile_send, returned, halos, wall_done
-    )
+    temp_next = call_heat(
+        potential_temp, wind_field, eddy_diff, facade_cell, tile_send, returned, halos
+    )
+    return (temp_next, wall_next)
 
 
 def solution(mesh):

time: 59.7 us -> 33.1 us (0.55)
  Pallas kernels: 58.8 us -> 29.9 us
  local copies, waits for them, and re-layouts: 0 us -> 2.26 us
    pallas_call x1, Pallas kernels: 34.4 us -> 5.42 us  [call_heat(): pl.pallas_call(heat_kernel, out_shape=jax.ShapeDtypeStruct(theta.shape, j...]
    unnamed x0 -> x1, local copies, waits for them, and re-layouts: none -> 2.26 us
where the time goes in v4:
time: 33.1 us; the launch traced here: 32.8 us
  Pallas kernels  29.9 us (90%)
  local copies, waits for them, and re-layouts  2.26 us (7%)
  between operations  0.65 us (2%)
    pallas_call x1, Pallas kernels, call_wall(): pl.pallas_call(functools.partial(wall_kernel, count, groups), out_shape=(...  20.3 us
    pallas_call x1, Pallas kernels, call_heat(): pl.pallas_call(heat_kernel, out_shape=jax.ShapeDtypeStruct(theta.shape, j...  5.42 us
    pallas_call x1, Pallas kernels, call_lookup(): pl.pallas_call(lookup_kernel, out_shape=jax.ShapeDtypeStruct((count, capa...  4.18 us
    unnamed x1, local copies, waits for them, and re-layouts  2.26 us

profile of v4, /device:TPU:0, one launch (start us, length us, event | category | flops | bytes accessed | tf_op | source)
XLA Modules:
  0.0 32.8 jit_solution(8805000752678385402)
XLA Ops:
  0.6 4.2 %lookup.1.listed_ref = f32[16,8,256]{2,1,0:T(8,128)} custom-call(f32[2,4,512]{2,1,0:T(4,128)} %theta_ref.1, f32[3,2,4,512]{3,2,1,0:T(4,128)} %wind_ref.1, s32[1,128,128]{2,1,0:T(8,128)} %cell_ref.1, s32[1,128]{1,0:T(1,128)} %send_ref.1), custom_call_target="tpu_custom_call" | custom-call | tf_op jit(solution)/shard_map/lookup/pallas_call | solution.py:163
  4.8 20.3 %wall.1 = (f32[1,64,32,128]{3,2,1,0:T(8,128)}, f32[16,8,128]{2,1,0:T(8,128)}, f32[2,512]{1,0:T(2,128)}, f32[2,512]{1,0:T(2,128)}, f32[4,512]{1,0:T(4,128)}, /*index=5*/f32[4,512]{1,0:T(4,128)}) custom-call(f32[16,8,256]{2,1,0:T(8,128)} %lookup.1.listed_ref, f32[2,4,512]{2,1,0:T(4,128)} %theta_ref.1, s32[1,64]{1,0:T(1,128)} %take_hbm.1, s32[1,64]{1,0:T(1,128)} %class_ref.1, ...), custom_call_target="tpu_custom_call" | custom-call | tf_op jit(solution)/shard_map/wall/pallas_call | solution.py:399
  25.1 5.4 %heat.1 = f32[2,4,512]{2,1,0:T(4,128)} custom-call(f32[2,4,512]{2,1,0:T(4,128)} %theta_ref.1, f32[3,2,4,512]{3,2,1,0:T(4,128)} %wind_ref.1, f32[2,4,512]{2,1,0:T(4,128)} %eddy_ref.1, s32[1,128,128]{2,1,0:T(8,128)} %cell_ref.1, s32[1,128]{1,0:T(1,128)} %send_ref.1, f32[16,8,128]{2,1,0:T(8,128)} %get-tuple-element.8.back_ref, ...), custom_call_target="tpu_custom_call" | custom-call | tf_op jit(solution)/shard_map/heat/pallas_call | solution.py:184
  30.5 2.3 %copy.14 = f32[1,64,32,128]{3,2,1,0:T(8,128)} copy(f32[1,64,32,128]{3,2,1,0:T(8,128)} %get-tuple-element.17) | data formatting | bytes 2097152
